TPU v7x, 512 devices: a whole 4x4x16 slice. The times are simulated.
512 devices in a mesh: ctx: 64 (over y, z), exp: 8 (over x, core).
Axes of the slice: x: 4, y: 4, z: 16, core: 2. Of those that a mesh axis runs over, the one named last changes fastest.
Arguments:
- patches: bfloat16 [8, 32768, 1280], P('exp', 'ctx'), may hold values from -36 to 300
- router: bfloat16 [1280, 32], replicated, may hold values from -1 to 1.1
- w_in: bfloat16 [32, 1280, 5120], P('exp', None, 'ctx'), may hold values from -0.15625 to 0.15625
- w_out: bfloat16 [32, 5120, 1280], P('exp', 'ctx'), may hold values from -0.078125 to 0.078125
Outputs:
- mixed: bfloat16 [8, 32768, 1280], P('exp', 'ctx')
All inputs are finite; a program needn't handle non-finite values.
Results may differ from a plain program's by a relative error of at most 0.012.
Values may be sent and summed in bfloat16 or wider, within the bound.
No kernel may reach another device: no remote copies, remote signals or barrier semaphores. Data moves between devices by JAX's collectives and lax.ppermute only.
A program may use at most 64 MiB of HBM per device.

v0:
```python
import jax
import jax.numpy as jnp
from jax import lax
from jax.sharding import PartitionSpec as P


def on_device(patches, router, w_in, w_out):
    rows = patches[0]
    logits = jnp.dot(rows, router, preferred_element_type=jnp.float32)
    local_max = jnp.max(logits, axis=0)
    slot_max = lax.pmax(local_max, "ctx")
    weights = jnp.exp(logits - slot_max[None, :])
    slot_total = lax.psum(jnp.sum(weights, axis=0), "ctx")
    dispatch = weights.astype(jnp.bfloat16)
    partial_sum = lax.dot_general(
        dispatch, rows, (((0,), (0,)), ((), ())), preferred_element_type=jnp.float32
    )
    own_count = w_in.shape[0]
    groups = router.shape[1] // own_count
    row_max = jnp.max(logits, axis=1, keepdims=True)
    combine = jnp.exp(logits - row_max)
    row_total = jnp.sum(combine, axis=1, keepdims=True)
    combine_low = combine.astype(jnp.bfloat16)
    summed = lax.psum(partial_sum, "ctx")
    slot_in = (summed / slot_total[:, None]).astype(jnp.bfloat16)
    arrived = lax.all_to_all(
        slot_in.reshape(groups, own_count, slot_in.shape[1]),
        "exp",
        split_axis=0,
        concat_axis=0,
        tiled=True,
    )
    hidden = jax.nn.gelu(
        jnp.einsum("bed,edf->bef", arrived, w_in, preferred_element_type=jnp.float32)
    ).astype(jnp.bfloat16)
    partial_out = jnp.einsum("bef,efd->bed", hidden, w_out, preferred_element_type=jnp.float32)
    out_sum = lax.psum(partial_out, "ctx").astype(jnp.bfloat16)
    slide_rows = lax.all_to_all(out_sum, "exp", split_axis=0, concat_axis=1, tiled=True)
    mixed = jnp.dot(combine_low, slide_rows[0], preferred_element_type=jnp.float32)
    return (mixed / row_total).astype(jnp.bfloat16)[None]


def solution(mesh):
    placed = (P("exp", "ctx", None), P(), P("exp", None, "ctx"), P("exp", "ctx", None))
    return jax.shard_map(
        on_device, mesh=mesh, in_specs=placed, out_specs=P("exp", "ctx", None), check_vma=False
    )
```

profile of v0, /device:TPU:6, one launch (start us, length us, event | category | flops | bytes accessed | tf_op | source)
XLA Modules:
  0.0 713.2 jit_solution(7605380070280773442)
XLA Ops:
  6.5 0.0 copy-start
  6.5 0.0 all-reduce.3.cloned.1.call-start
  6.5 1.3 copy-done
  7.9 1.5 fusion.37
  9.3 0.0 copy-start.1
  9.4 0.0 copy-start.2
  9.4 150.0 %pmax.7 = f32[32]{0:T(128)S(1)} all-reduce(f32[32]{0:T(128)S(1)} %get-tuple-element.8), channel_id=1, replica_groups=mesh['ctx'=64,'exp'=8] {'ctx'}, use_global_device_ids=true, to_apply=%region_2.0 | all-reduce | flops 32 | bytes 256 | tf_op jit(solution)/shard_map/pmax | solution.py:11
  159.4 1.0 fusion.2
  160.4 0.0 all-reduce.3.cloned.1.call-update
  160.5 0.2 fusion.7
  160.7 138.0 %psum.22 = f32[32]{0:T(128)S(1)} all-reduce(f32[32]{0:T(128)S(1)} %get-tuple-element.6), channel_id=1, replica_groups=mesh['ctx'=64,'exp'=8] {'ctx'}, use_global_device_ids=true, to_apply=%region_5.0 | all-reduce | flops 32 | bytes 256 | tf_op jit(solution)/shard_map/psum | solution.py:13
  298.6 111.4 %all-reduce.3.cloned.1.call-done = f32[32,1280]{1,0:T(8,128)} async-done(((f32[32,1280]{1,0:T(8,128)}), f32[32,1280]{1,0:T(8,128)}) %all-reduce.3.cloned.1.call-update) | async-done | bytes 163856 | tf_op jit(solution)/shard_map/psum | solution.py:24
  410.1 1.0 divide_convert_fusion
  411.1 8.2 %all_to_all.14 = bf16[8,4,1280]{2,1,0:T(4,128)(2,1)S(1)} all-to-all(bf16[8,4,1280]{2,1,0:T(4,128)(2,1)S(1)} %reshape.11), channel_id=1, replica_groups=mesh['ctx'=64,'exp'=8] {'exp'}, dimensions={0} | all-to-all | bytes 163840 | tf_op jit(solution)/shard_map/all_to_all | solution.py:26
  419.3 0.0 copy-done.1
  419.3 0.0 copy-done.2
  419.3 0.5 convolution_bitcast_fusion
  419.8 276.8 %all-reduce.4 = bf16[8,4,1280]{2,0,1:T(8,128)(2,1)S(1)} all-reduce(f32[8,4,1280]{2,0,1:T(8,128)S(1)} %convolution_bitcast_fusion), channel_id=1, replica_groups=mesh['ctx'=64,'exp'=8] {'ctx'}, use_global_device_ids=true, to_apply=%region_6.0 | all-reduce | flops 40960 | bytes 245760 | tf_op jit(solution)/shard_map/psum | solution.py:37
  696.6 8.1 %all_to_all.15 = bf16[8,4,1280]{2,1,0:T(4,128)(2,1)S(1)} all-to-all(bf16[8,4,1280]{2,1,0:T(4,128)(2,1)S(1)} %copy.9), channel_id=1, replica_groups=mesh['ctx'=64,'exp'=8] {'exp'}, dimensions={0} | all-to-all | bytes 163840 | tf_op jit(solution)/shard_map/all_to_all | solution.py:38
  704.7 1.6 fusion.1
  (3 shorter events, 0.1 us)
Async XLA Ops:
  6.5 1.3 copy-start
  6.5 403.5 %all-reduce.3.cloned.1.call-start = ((), (), s32[]{:S(2)}) async-start(), calls=%async_computation.2 | async-start | bytes 327680 | tf_op jit(solution)/shard_map/psum | solution.py:24
  9.3 410.0 %copy-start.1 = (bf16[4,80,1280]{2,1,0:T(8,128)(2,1)S(1)}, bf16[4,80,1280]{2,1,0:T(8,128)(2,1)}, u32[]{:S(2)}) copy-start(bf16[4,80,1280]{2,1,0:T(8,128)(2,1)} %param.7) | copy-start | bytes 2457604
  9.4 410.0 %copy-start.2 = (bf16[4,1280,80]{1,2,0:T(8,128)(2,1)S(1)}, bf16[4,1280,80]{1,2,0:T(8,128)(2,1)}, u32[]{:S(2)}) copy-start(bf16[4,1280,80]{1,2,0:T(8,128)(2,1)} %param.6) | copy-start | bytes 2457604
Sparse Core Ops, SparseCore 0:
  160.6 249.4 all-reduce.2
where the time goes:
time: 716 us; the launch traced here: 713 us
  blocking collectives  581 us (81%)
  waiting for transfers between devices  111 us (16%)
  between operations  13.4 us (2%)
    psum x1, blocking collectives, on_device(): out_sum = lax.psum(partial_out, 'ctx').astype(jnp.bfloat16)  277 us
    pmax x1, blocking collectives, on_device(): slot_max = lax.pmax(local_max, 'ctx')  150 us
    psum x1, blocking collectives, on_device(): slot_total = lax.psum(jnp.sum(weights, axis=0), 'ctx')  138 us
    psum x1, waiting for transfers between devices, on_device(): summed = lax.psum(partial_sum, 'ctx')  111 us
  transfers between devices with their start and end apart: 1, of which 1 were waited for; matrix products, arithmetic and copies ran while one was open for 0% of the time, Pallas kernels for 0%

commit v1 on v0

v1 whole, which is shorter than its diff:
```python
import jax
import jax.numpy as jnp
from jax import lax
from jax.sharding import Mesh, PartitionSpec as P

Y, Z, X, C = 4, 16, 4, 2
ZL = 1
ZH = Z // ZL
LANES = 384
BF = jnp.bfloat16
F32 = jnp.float32
NEAR = ("y", "zl", "x", "c")


def exact_parts(v):
    high = lax.reduce_precision(v, 8, 7)
    rest = v - high
    mid = lax.reduce_precision(rest, 8, 7)
    low = rest - mid
    return jnp.stack([high, mid, low], axis=-1).astype(BF)


def packed(mean, lse):
    pad = LANES - mean.shape[-1] - 3
    tail = jnp.pad(exact_parts(lse), [(0, 0)] * lse.ndim + [(0, pad)])
    tail = jnp.broadcast_to(tail, mean.shape[:-1] + (tail.shape[-1],))
    return jnp.concatenate([mean.astype(BF), tail], axis=-1)


def merged(pieces, width):
    mean = pieces[..., :width].astype(F32)
    lse = jnp.sum(pieces[..., width : width + 3].astype(F32), axis=-1)
    top = jnp.max(lse, axis=0)
    weight = jnp.exp(lse - top)
    total = jnp.sum(weight, axis=0)
    mean = jnp.sum(mean * weight[..., None], axis=0) / total[..., None]
    return mean, top + jnp.log(total)


def spread(block, axes, count):
    copies = jnp.broadcast_to(block[None], (count,) + block.shape)
    return lax.all_to_all(copies, axes, 0, 0, tiled=True)


def on_device(patches, router, w_in, w_out):
    rows = patches[0]
    own = w_in.shape[0]
    slots = router.shape[1]
    groups = slots // own
    depth = rows.shape[1]
    width = depth // Y
    part = own // ZL

    logits = jnp.dot(rows, router, preferred_element_type=F32)
    local_max = jnp.max(logits, axis=0)
    weights = jnp.exp(logits - local_max[None, :])
    local_total = jnp.sum(weights, axis=0)
    local_sum = lax.dot_general(
        weights.astype(BF), rows, (((0,), (0,)), ((), ())), preferred_element_type=F32
    )
    mean = local_sum / local_total[:, None]
    lse = local_max + jnp.log(local_total)

    mean = mean.reshape(groups, ZL, part, Y, width).transpose(3, 1, 0, 2, 4)
    lse = lse.reshape(1, groups, ZL, part).transpose(0, 2, 1, 3)
    pieces = packed(mean, lse).reshape(Y * ZL * groups, part, LANES)
    got = lax.all_to_all(pieces, NEAR, 0, 0, tiled=True)
    mean, lse = merged(got.reshape(Y * ZL, groups * part, LANES), width)
    got = spread(packed(mean, lse), "zh", ZH)
    mean, _ = merged(got, width)
    got = spread(mean.astype(BF), ("y", "zl"), Y * ZL)
    slot_in = got.reshape(Y, ZL, groups, part, width).transpose(2, 1, 3, 0, 4).reshape(groups, own, depth)

    hidden = jax.nn.gelu(jnp.einsum("bed,edf->bef", slot_in, w_in, preferred_element_type=F32)).astype(BF)
    partial_out = jnp.einsum("bef,efd->bed", hidden, w_out, preferred_element_type=F32).astype(BF)

    pieces = partial_out.reshape(groups, ZL, part, Y, width).transpose(3, 1, 0, 2, 4)
    got = lax.all_to_all(pieces.reshape(Y * ZL * groups, part, width), NEAR, 0, 0, tiled=True)
    total = jnp.sum(got.reshape(Y * ZL, groups * part, width).astype(F32), axis=0).astype(BF)
    got = spread(total, "zh", ZH)
    total = jnp.sum(got.astype(F32), axis=0).astype(BF)
    got = spread(total, ("y", "zl"), Y * ZL)
    slot_out = got.reshape(Y, ZL, groups, part, width).transpose(2, 1, 3, 0, 4).reshape(slots, depth)

    row_max = jnp.max(logits, axis=1, keepdims=True)
    combine = jnp.exp(logits - row_max)
    row_total = jnp.sum(combine, axis=1, keepdims=True)
    mixed = jnp.dot(combine.astype(BF), slot_out, preferred_element_type=F32)
    return (mixed / row_total).astype(BF)[None]


def solution(mesh):
    fine = Mesh(mesh.devices.reshape(Y, ZH, ZL, X, C), ("y", "zh", "zl", "x", "c"))
    ctx, exp = ("y", "zh", "zl"), ("x", "c")
    placed = (P(exp, ctx, None), P(), P(exp, None, ctx), P(exp, ctx, None))
    return jax.shard_map(
        on_device, mesh=fine, in_specs=placed, out_specs=P(exp, ctx, None), check_vma=False
    )
```

time: 716 us -> 120 us (0.17)
  blocking collectives: 581 us -> 110 us
  waiting for transfers between devices: 111 us -> 0 us
  between operations: 13.4 us -> 0.21 us
    psum x2 -> x0, blocking collectives: 415 us -> none  [the longest x1 277 us: on_device(): out_sum = lax.psum(partial_out, 'ctx').astype(jnp.bfloat16)]
    pmax x1 -> x0, blocking collectives: 150 us -> none  [on_device(): slot_max = lax.pmax(local_max, 'ctx')]
    psum x1 -> x0, waiting for transfers between devices: 111 us -> none  [on_device(): summed = lax.psum(partial_sum, 'ctx')]
    all_to_all x2 -> x6, blocking collectives: 16.3 us -> 110 us  [the longest x4 84.4 us: spread(): return lax.all_to_all(copies, axes, 0, 0, tiled=True)]
  transfers between devices with their start and end apart: 1 -> 0, of which waited for: 1 -> 0; matrix products, arithmetic and copies ran while one was open for 0% -> 0% of each run, Pallas kernels for 0% -> 0%
where the time goes in v1:
time: 120 us; the launch traced here: 119 us
  blocking collectives  110 us (92%)
  matrix products  3.95 us (3%)
  local copies, waits for them, and re-layouts  3.14 us (3%)
  other arithmetic  1.7 us (1%)
    all_to_all x4, blocking collectives, spread(): return lax.all_to_all(copies, axes, 0, 0, tiled=True)  84.4 us
    all_to_all x1, blocking collectives, on_device(): got = lax.all_to_all(pieces, NEAR, 0, 0, tiled=True)  14.4 us
    all_to_all x1, blocking collectives, on_device(): lax.all_to_all(pieces.reshape(Y * ZL * groups, part, width), NEAR, 0, 0,...  10.9 us

profile of v1, /device:TPU:6, one launch (start us, length us, event | category | flops | bytes accessed | tf_op | source)
XLA Modules:
  0.0 118.6 jit_solution(6875886981409166038)
XLA Ops:
  0.0 1.3 %copy-done = bf16[1,512,1280]{2,1,0:T(8,128)(2,1)S(1)} copy-done((bf16[1,512,1280]{2,1,0:T(8,128)(2,1)S(1)}, bf16[1,512,1280]{2,1,0:T(8,128)(2,1)}, u32[]{:S(2)}) %copy-start) | copy-done | bytes 1310744
  1.3 1.5 %fusion.48 = (f32[512]{0:T(512)S(1)}, f32[32]{0:T(128)S(1)}, f32[512,32]{0,1:T(8,128)S(1)}) fusion(bf16[1280,32]{0,1:T(8,128)(2,1)} %param.5, bf16[1,512,1280]{2,1,0:T(8,128)(2,1)S(1)} %copy-done), kind=kOutput, calls=%fused_computation.71 | convolution fusion | flops 41975264 | bytes 1460352 | tf_op jit(solution)/shard_map/dot_general | solution.py:54
  2.8 0.7 fusion.14
  3.5 0.4 fusion.2
  3.9 0.1 copy.41
  4.0 0.1 copy.43
  4.1 0.1 copy.42
  4.4 0.2 convert_element_type.70
  4.7 14.4 %all_to_all.30 = bf16[32,4,384]{2,1,0:T(4,128)(2,1)S(1)} all-to-all(bf16[32,4,384]{2,1,0:T(4,128)(2,1)S(1)} %copy.45), channel_id=1, replica_groups=mesh['y'=4,'zh'=16,'zl'=1,'x'=4,'c'=2] {'y','zl','x','c'}, dimensions={0} | all-to-all | bytes 196608 | tf_op jit(solution)/shard_map/all_to_all | solution.py:67
  19.1 0.2 convert_reduce_fusion
  19.5 0.1 copy.55
  19.8 38.2 %all_to_all.31 = bf16[16,32,384]{2,1,0:T(8,128)(2,1)S(1)} all-to-all(bf16[16,32,384]{2,1,0:T(8,128)(2,1)S(1)} %broadcast_in_dim.16), channel_id=1, replica_groups=mesh['y'=4,'zh'=16,'zl'=1,'x'=4,'c'=2] {'zh'}, dimensions={0} | all-to-all | bytes 786432 | tf_op jit(solution)/shard_map/all_to_all | solution.py:42
  58.0 0.1 slice.19
  58.1 0.2 copy.47
  58.3 0.2 multiply_reduce_fusion
  58.6 8.2 %all_to_all.32 = bf16[4,32,320]{2,1,0:T(8,128)(2,1)S(1)} all-to-all(bf16[4,32,320]{2,1,0:T(8,128)(2,1)S(1)} %broadcast_in_dim.17), channel_id=1, replica_groups=mesh['y'=4,'zh'=16,'zl'=1,'x'=4,'c'=2] {'y','zl'}, dimensions={0} | all-to-all | bytes 163840 | tf_op jit(solution)/shard_map/all_to_all | solution.py:42
  66.8 0.1 reshape.288
  67.0 0.5 fusion.3
  67.5 0.2 reshape.283
  67.7 10.9 %all_to_all.33 = bf16[32,4,320]{2,1,0:T(4,128)(2,1)S(1)} all-to-all(bf16[32,4,320]{2,1,0:T(4,128)(2,1)S(1)} %copy.51), channel_id=1, replica_groups=mesh['y'=4,'zh'=16,'zl'=1,'x'=4,'c'=2] {'y','zl','x','c'}, dimensions={0} | all-to-all | bytes 163840 | tf_op jit(solution)/shard_map/all_to_all | solution.py:78
  78.7 29.8 %all_to_all.34 = bf16[16,32,320]{2,1,0:T(8,128)(2,1)S(1)} all-to-all(bf16[16,32,320]{2,1,0:T(8,128)(2,1)S(1)} %broadcast_in_dim.18), channel_id=1, replica_groups=mesh['y'=4,'zh'=16,'zl'=1,'x'=4,'c'=2] {'zh'}, dimensions={0} | all-to-all | bytes 655360 | tf_op jit(solution)/shard_map/all_to_all | solution.py:42
  108.7 8.2 %all_to_all.35 = bf16[4,32,320]{2,1,0:T(8,128)(2,1)S(1)} all-to-all(bf16[4,32,320]{2,1,0:T(8,128)(2,1)S(1)} %broadcast_in_dim.19), channel_id=1, replica_groups=mesh['y'=4,'zh'=16,'zl'=1,'x'=4,'c'=2] {'y','zl'}, dimensions={0} | all-to-all | bytes 163840 | tf_op jit(solution)/shard_map/all_to_all | solution.py:42
  116.9 0.1 reshape.287
  117.0 1.6 %fusion.1 = bf16[1,512,1280]{2,1,0:T(8,128)(2,1)} fusion(bf16[32,1280]{1,0:T(8,128)(2,1)S(1)} %reshape.287, f32[512]{0:T(512)S(1)} %copy-done.3, f32[512,32]{0,1:T(8,128)S(1)} %get-tuple-element.19, f32[512]{0:T(512)S(1)} %get-tuple-element.7), kind=kOutput, calls=%fused_computation.2 | convolution fusion | flops 43286528 | bytes 1462272 | tf_op jit(solution)/shard_map/dot_general | solution.py:88
  (39 shorter events, 1.3 us)
Async XLA Ops:
  0.0 1.3 %copy-start = (bf16[1,512,1280]{2,1,0:T(8,128)(2,1)S(1)}, bf16[1,512,1280]{2,1,0:T(8,128)(2,1)}, u32[]{:S(2)}) copy-start(bf16[1,512,1280]{2,1,0:T(8,128)(2,1)} %param.4) | copy-start | bytes 3932164
  19.8 47.2 %copy-start.1 = (bf16[4,80,1280]{2,1,0:T(8,128)(2,1)S(1)}, bf16[4,80,1280]{2,1,0:T(8,128)(2,1)}, u32[]{:S(2)}) copy-start(bf16[4,80,1280]{2,1,0:T(8,128)(2,1)} %param.7) | copy-start | bytes 2457604
  19.8 47.2 %copy-start.2 = (bf16[4,1280,80]{1,2,0:T(8,128)(2,1)S(1)}, bf16[4,1280,80]{1,2,0:T(8,128)(2,1)}, u32[]{:S(2)}) copy-start(bf16[4,1280,80]{1,2,0:T(8,128)(2,1)} %param.6) | copy-start | bytes 2457604
  78.6 38.4 %copy-start.3 = (f32[512]{0:T(512)S(1)}, f32[512]{0:T(512)}, u32[]{:S(2)}) copy-start(f32[512]{0:T(512)} %get-tuple-element.5) | copy-start | bytes 6148

commit v2 on v1

--- a/solution.py
+++ b/solution.py
@@ -4,7 +4,7 @@
 from jax.sharding import Mesh, PartitionSpec as P
 
 Y, Z, X, C = 4, 16, 4, 2
-ZL = 1
+ZL = 2
 ZH = Z // ZL
 LANES = 384
 BF = jnp.bfloat16

time: 120 us -> 102 us (0.85)
  blocking collectives: 110 us -> 92.8 us
    all_to_all x4, blocking collectives: 84.4 us -> 64.5 us  [spread(): return lax.all_to_all(copies, axes, 0, 0, tiled=True)]
    all_to_all x1, blocking collectives: 14.4 us -> 16 us  [on_device(): got = lax.all_to_all(pieces, NEAR, 0, 0, tiled=True)]
    all_to_all x1, blocking collectives: 10.9 us -> 12.3 us  [on_device(): lax.all_to_all(pieces.reshape(Y * ZL * groups, part, width), NEAR, 0, 0,...]
where the time goes in v2:
time: 102 us; the launch traced here: 101 us
  blocking collectives  92.8 us (91%)
  matrix products  3.96 us (4%)
  local copies, waits for them, and re-layouts  3.09 us (3%)
  other arithmetic  1.09 us (1%)
    all_to_all x4, blocking collectives, spread(): return lax.all_to_all(copies, axes, 0, 0, tiled=True)  64.5 us
    all_to_all x1, blocking collectives, on_device(): got = lax.all_to_all(pieces, NEAR, 0, 0, tiled=True)  16 us
    all_to_all x1, blocking collectives, on_device(): lax.all_to_all(pieces.reshape(Y * ZL * groups, part, width), NEAR, 0, 0,...  12.3 us

profile of v2, /device:TPU:6, one launch (start us, length us, event | category | flops | bytes accessed | tf_op | source)
XLA Modules:
  0.0 101.2 jit_solution(10788739709812721224)
XLA Ops:
  0.0 1.3 %copy-done = bf16[1,512,1280]{2,1,0:T(8,128)(2,1)S(1)} copy-done((bf16[1,512,1280]{2,1,0:T(8,128)(2,1)S(1)}, bf16[1,512,1280]{2,1,0:T(8,128)(2,1)}, u32[]{:S(2)}) %copy-start) | copy-done | bytes 1310744
  1.3 1.5 %fusion.44 = (f32[512]{0:T(512)S(1)}, f32[32]{0:T(128)S(1)}, f32[512,32]{0,1:T(8,128)S(1)}) fusion(bf16[1280,32]{0,1:T(8,128)(2,1)} %param.5, bf16[1,512,1280]{2,1,0:T(8,128)(2,1)S(1)} %copy-done), kind=kOutput, calls=%fused_computation.72 | convolution fusion | flops 41975264 | bytes 1460352 | tf_op jit(solution)/shard_map/dot_general | solution.py:54
  2.8 0.2 fusion.13
  3.0 0.4 fusion.2
  3.4 0.1 add.48
  3.5 0.1 copy.63
  3.7 0.2 convert_element_type.70
  4.1 0.1 copy.65
  4.2 16.0 %all_to_all.30 = bf16[64,2,384]{2,1,0:T(2,128)(2,1)S(1)} all-to-all(bf16[64,2,384]{2,1,0:T(2,128)(2,1)S(1)} %copy.65), channel_id=1, replica_groups=mesh['y'=4,'zh'=8,'zl'=2,'x'=4,'c'=2] {'y','zl','x','c'}, dimensions={0} | all-to-all | bytes 196608 | tf_op jit(solution)/shard_map/all_to_all | solution.py:67
  20.2 0.2 convert_reduce_fusion
  20.6 0.1 copy.73
  20.8 28.5 %all_to_all.31 = bf16[8,16,384]{2,1,0:T(8,128)(2,1)S(1)} all-to-all(bf16[8,16,384]{2,1,0:T(8,128)(2,1)S(1)} %broadcast_in_dim.16), channel_id=1, replica_groups=mesh['y'=4,'zh'=8,'zl'=2,'x'=4,'c'=2] {'zh'}, dimensions={0} | all-to-all | bytes 196608 | tf_op jit(solution)/shard_map/all_to_all | solution.py:42
  49.4 0.1 copy.72
  49.6 0.1 multiply_reduce_fusion
  49.8 9.5 %all_to_all.32 = bf16[8,16,320]{2,1,0:T(8,128)(2,1)S(1)} all-to-all(bf16[8,16,320]{2,1,0:T(8,128)(2,1)S(1)} %broadcast_in_dim.17), channel_id=1, replica_groups=mesh['y'=4,'zh'=8,'zl'=2,'x'=4,'c'=2] {'y','zl'}, dimensions={0} | all-to-all | bytes 163840 | tf_op jit(solution)/shard_map/all_to_all | solution.py:42
  59.4 0.1 reshape.207
  59.6 0.5 fusion.3
  60.0 0.2 reshape.208
  60.2 0.1 copy.70
  60.3 12.3 %all_to_all.33 = bf16[64,2,320]{2,1,0:T(2,128)(2,1)S(1)} all-to-all(bf16[64,2,320]{2,1,0:T(2,128)(2,1)S(1)} %copy.70), channel_id=1, replica_groups=mesh['y'=4,'zh'=8,'zl'=2,'x'=4,'c'=2] {'y','zl','x','c'}, dimensions={0} | all-to-all | bytes 163840 | tf_op jit(solution)/shard_map/all_to_all | solution.py:78
  72.8 17.2 %all_to_all.34 = bf16[8,16,320]{2,1,0:T(8,128)(2,1)S(1)} all-to-all(bf16[8,16,320]{2,1,0:T(8,128)(2,1)S(1)} %broadcast_in_dim.18), channel_id=1, replica_groups=mesh['y'=4,'zh'=8,'zl'=2,'x'=4,'c'=2] {'zh'}, dimensions={0} | all-to-all | bytes 163840 | tf_op jit(solution)/shard_map/all_to_all | solution.py:42
  90.0 9.4 %all_to_all.35 = bf16[8,16,320]{2,1,0:T(8,128)(2,1)S(1)} all-to-all(bf16[8,16,320]{2,1,0:T(8,128)(2,1)S(1)} %broadcast_in_dim.19), channel_id=1, replica_groups=mesh['y'=4,'zh'=8,'zl'=2,'x'=4,'c'=2] {'y','zl'}, dimensions={0} | all-to-all | bytes 163840 | tf_op jit(solution)/shard_map/all_to_all | solution.py:42
  99.5 0.1 reshape.212
  99.6 1.6 %fusion.1 = bf16[1,512,1280]{2,1,0:T(8,128)(2,1)} fusion(bf16[32,1280]{1,0:T(8,128)(2,1)S(1)} %reshape.212, f32[512]{0:T(512)S(1)} %get-tuple-element.5, f32[512,32]{0,1:T(8,128)S(1)} %get-tuple-element.19, f32[512]{0:T(512)S(1)} %get-tuple-element.7), kind=kOutput, calls=%fused_computation.2 | convolution fusion | flops 43286528 | bytes 1462272 | tf_op jit(solution)/shard_map/dot_general | solution.py:88
  (37 shorter events, 1.2 us)
Async XLA Ops:
  0.0 1.3 %copy-start = (bf16[1,512,1280]{2,1,0:T(8,128)(2,1)S(1)}, bf16[1,512,1280]{2,1,0:T(8,128)(2,1)}, u32[]{:S(2)}) copy-start(bf16[1,512,1280]{2,1,0:T(8,128)(2,1)} %param.4) | copy-start | bytes 3932164
  3.9 55.6 %copy-start.1 = (bf16[4,80,1280]{2,1,0:T(8,128)(2,1)S(1)}, bf16[4,80,1280]{2,1,0:T(8,128)(2,1)}, u32[]{:S(2)}) copy-start(bf16[4,80,1280]{2,1,0:T(8,128)(2,1)} %param.7) | copy-start | bytes 2457604
  3.9 55.6 %copy-start.2 = (bf16[4,1280,80]{1,2,0:T(8,128)(2,1)S(1)}, bf16[4,1280,80]{1,2,0:T(8,128)(2,1)}, u32[]{:S(2)}) copy-start(bf16[4,1280,80]{1,2,0:T(8,128)(2,1)} %param.6) | copy-start | bytes 2457604

commit v3 on v2

--- a/solution.py
+++ b/solution.py
@@ -6,7 +6,7 @@
 Y, Z, X, C = 4, 16, 4, 2
 ZL = 2
 ZH = Z // ZL
-LANES = 384
+LANES = 768
 BF = jnp.bfloat16
 F32 = jnp.float32
 NEAR = ("y", "zl", "x", "c")
@@ -48,8 +48,7 @@
     slots = router.shape[1]
     groups = slots // own
     depth = rows.shape[1]
-    width = depth // Y
-    part = own // ZL
+    width = depth // ZL
 
     logits = jnp.dot(rows, router, preferred_element_type=F32)
     local_max = jnp.max(logits, axis=0)
@@ -61,26 +60,26 @@
     mean = local_sum / local_total[:, None]
     lse = local_max + jnp.log(local_total)
 
-    mean = mean.reshape(groups, ZL, part, Y, width).transpose(3, 1, 0, 2, 4)
-    lse = lse.reshape(1, groups, ZL, part).transpose(0, 2, 1, 3)
-    pieces = packed(mean, lse).reshape(Y * ZL * groups, part, LANES)
+    mean = mean.reshape(groups, Y, ZL, width).transpose(1, 2, 0, 3)
+    lse = jnp.broadcast_to(lse.reshape(groups, Y).T[:, None], (Y, ZL, groups))
+    pieces = packed(mean, lse).reshape(Y * ZL * groups, LANES)
     got = lax.all_to_all(pieces, NEAR, 0, 0, tiled=True)
-    mean, lse = merged(got.reshape(Y * ZL, groups * part, LANES), width)
+    mean, lse = merged(got.reshape(Y * ZL, groups, LANES), width)
     got = spread(packed(mean, lse), "zh", ZH)
     mean, _ = merged(got, width)
     got = spread(mean.astype(BF), ("y", "zl"), Y * ZL)
-    slot_in = got.reshape(Y, ZL, groups, part, width).transpose(2, 1, 3, 0, 4).reshape(groups, own, depth)
+    slot_in = got.reshape(Y, ZL, groups, width).transpose(2, 0, 1, 3).reshape(groups, own, depth)
 
     hidden = jax.nn.gelu(jnp.einsum("bed,edf->bef", slot_in, w_in, preferred_element_type=F32)).astype(BF)
     partial_out = jnp.einsum("bef,efd->bed", hidden, w_out, preferred_element_type=F32).astype(BF)
 
-    pieces = partial_out.reshape(groups, ZL, part, Y, width).transpose(3, 1, 0, 2, 4)
-    got = lax.all_to_all(pieces.reshape(Y * ZL * groups, part, width), NEAR, 0, 0, tiled=True)
-    total = jnp.sum(got.reshape(Y * ZL, groups * part, width).astype(F32), axis=0).astype(BF)
+    pieces = partial_out.reshape(groups, Y, ZL, width).transpose(1, 2, 0, 3)
+    got = lax.all_to_all(pieces.reshape(Y * ZL * groups, width), NEAR, 0, 0, tiled=True)
+    total = jnp.sum(got.reshape(Y * ZL, groups, width).astype(F32), axis=0).astype(BF)
     got = spread(total, "zh", ZH)
     total = jnp.sum(got.astype(F32), axis=0).astype(BF)
     got = spread(total, ("y", "zl"), Y * ZL)
-    slot_out = got.reshape(Y, ZL, groups, part, width).transpose(2, 1, 3, 0, 4).reshape(slots, depth)
+    slot_out = got.reshape(Y, ZL, groups, width).transpose(2, 0, 1, 3).reshape(slots, depth)
 
     row_max = jnp.max(logits, axis=1, keepdims=True)
     combine = jnp.exp(logits - row_max)

time: 102 us -> 102 us (level)
  other arithmetic: 1.09 us -> 2.15 us
    all_to_all x0 -> x2, other arithmetic: none -> 1.34 us  [the longest x1 0.68 us: on_device(): lax.all_to_all(pieces.reshape(Y * ZL * groups, width), NEAR, 0, 0, tiled=...]
where the time goes in v3:
time: 102 us; the launch traced here: 101 us
  blocking collectives  91.8 us (90%)
  matrix products  3.96 us (4%)
  local copies, waits for them, and re-layouts  3.14 us (3%)
  other arithmetic  2.15 us (2%)
    all_to_all x4, blocking collectives, spread(): return lax.all_to_all(copies, axes, 0, 0, tiled=True)  63.6 us
    all_to_all x1, blocking collectives, on_device(): got = lax.all_to_all(pieces, NEAR, 0, 0, tiled=True)  15.9 us
    all_to_all x1, blocking collectives, on_device(): lax.all_to_all(pieces.reshape(Y * ZL * groups, width), NEAR, 0, 0, tiled=...  12.3 us

profile of v3, /device:TPU:6, one launch (start us, length us, event | category | flops | bytes accessed | tf_op | source)
XLA Modules:
  0.0 101.2 jit_solution(7846706291232019910)
XLA Ops:
  0.0 1.3 %copy-done = bf16[1,512,1280]{2,1,0:T(8,128)(2,1)S(1)} copy-done((bf16[1,512,1280]{2,1,0:T(8,128)(2,1)S(1)}, bf16[1,512,1280]{2,1,0:T(8,128)(2,1)}, u32[]{:S(2)}) %copy-start) | copy-done | bytes 1310744
  1.3 1.5 %fusion.36 = (f32[512]{0:T(512)S(1)}, f32[32]{0:T(128)S(1)}, f32[512,32]{0,1:T(8,128)S(1)}) fusion(bf16[1280,32]{0,1:T(8,128)(2,1)} %param.5, bf16[1,512,1280]{2,1,0:T(8,128)(2,1)S(1)} %copy-done), kind=kOutput, calls=%fused_computation.66 | convolution fusion | flops 41975264 | bytes 1460352 | tf_op jit(solution)/shard_map/dot_general | solution.py:53
  2.8 0.2 fusion.8
  3.0 0.4 fusion.2
  3.5 0.1 copy.49
  3.6 0.1 copy.51
  3.7 0.1 copy.50
  3.8 0.1 copy.52
  4.0 0.5 broadcast.51
  4.6 0.7 reduce.2
  5.3 15.9 %all_to_all.38 = bf16[64,2,384]{2,1,0:T(2,128)(2,1)S(1)} all-to-all(bf16[64,2,384]{2,1,0:T(2,128)(2,1)S(1)} %reshape.143), channel_id=1, replica_groups=mesh['y'=4,'zh'=8,'zl'=2,'x'=4,'c'=2] {'y','zl','x','c'}, dimensions={0} | all-to-all | bytes 196608 | tf_op jit(solution)/shard_map/all_to_all | solution.py:66
  21.4 0.1 multiply_reduce_fusion.1
  21.6 0.1 copy.61
  21.7 28.5 %all_to_all.39 = bf16[8,8,768]{2,1,0:T(8,128)(2,1)S(1)} all-to-all(bf16[8,8,768]{2,1,0:T(8,128)(2,1)S(1)} %broadcast_in_dim.10), channel_id=1, replica_groups=mesh['y'=4,'zh'=8,'zl'=2,'x'=4,'c'=2] {'zh'}, dimensions={0} | all-to-all | bytes 196608 | tf_op jit(solution)/shard_map/all_to_all | solution.py:42
  50.2 0.1 copy.60
  50.6 9.4 %all_to_all.40 = bf16[8,8,640]{2,1,0:T(8,128)(2,1)S(1)} all-to-all(bf16[8,8,640]{2,1,0:T(8,128)(2,1)S(1)} %broadcast_in_dim.11), channel_id=1, replica_groups=mesh['y'=4,'zh'=8,'zl'=2,'x'=4,'c'=2] {'y','zl'}, dimensions={0} | all-to-all | bytes 163840 | tf_op jit(solution)/shard_map/all_to_all | solution.py:42
  60.0 0.5 convolution_convert_fusion
  60.4 0.7 reduce.3
  61.1 0.1 reshape.145
  61.3 12.3 %all_to_all.41 = bf16[64,2,320]{2,1,0:T(2,128)(2,1)S(1)} all-to-all(bf16[64,2,320]{2,1,0:T(2,128)(2,1)S(1)} %reshape.145), channel_id=1, replica_groups=mesh['y'=4,'zh'=8,'zl'=2,'x'=4,'c'=2] {'y','zl','x','c'}, dimensions={0} | all-to-all | bytes 163840 | tf_op jit(solution)/shard_map/all_to_all | solution.py:77
  73.6 0.2 reshape.146
  73.8 16.9 %all_to_all.42 = bf16[8,8,640]{2,1,0:T(8,128)(2,1)S(1)} all-to-all(bf16[8,8,640]{2,1,0:T(8,128)(2,1)S(1)} %broadcast_in_dim.12), channel_id=1, replica_groups=mesh['y'=4,'zh'=8,'zl'=2,'x'=4,'c'=2] {'zh'}, dimensions={0} | all-to-all | bytes 163840 | tf_op jit(solution)/shard_map/all_to_all | solution.py:42
  90.7 8.8 %all_to_all.43 = bf16[8,8,640]{2,1,0:T(8,128)(2,1)S(1)} all-to-all(bf16[8,8,640]{2,1,0:T(8,128)(2,1)S(1)} %broadcast_in_dim.13), channel_id=1, replica_groups=mesh['y'=4,'zh'=8,'zl'=2,'x'=4,'c'=2] {'y','zl'}, dimensions={0} | all-to-all | bytes 163840 | tf_op jit(solution)/shard_map/all_to_all | solution.py:42
  99.6 1.6 %fusion.1 = bf16[1,512,1280]{2,1,0:T(8,128)(2,1)} fusion(bf16[32,1280]{1,0:T(8,128)(2,1)S(1)} %bitcast.70, f32[512]{0:T(512)S(1)} %get-tuple-element.5, f32[512,32]{0,1:T(8,128)S(1)} %get-tuple-element.19, f32[512]{0:T(512)S(1)} %get-tuple-element.7), kind=kOutput, calls=%fused_computation.2 | convolution fusion | flops 43286528 | bytes 1462272 | tf_op jit(solution)/shard_map/dot_general | solution.py:87
  (39 shorter events, 0.9 us)
Async XLA Ops:
  0.0 1.3 %copy-start = (bf16[1,512,1280]{2,1,0:T(8,128)(2,1)S(1)}, bf16[1,512,1280]{2,1,0:T(8,128)(2,1)}, u32[]{:S(2)}) copy-start(bf16[1,512,1280]{2,1,0:T(8,128)(2,1)} %param.4) | copy-start | bytes 3932164
  4.0 56.0 %copy-start.1 = (bf16[4,80,1280]{2,1,0:T(8,128)(2,1)S(1)}, bf16[4,80,1280]{2,1,0:T(8,128)(2,1)}, u32[]{:S(2)}) copy-start(bf16[4,80,1280]{2,1,0:T(8,128)(2,1)} %param.7) | copy-start | bytes 2457604
  4.0 56.0 %copy-start.2 = (bf16[4,1280,80]{1,2,0:T(8,128)(2,1)S(1)}, bf16[4,1280,80]{1,2,0:T(8,128)(2,1)}, u32[]{:S(2)}) copy-start(bf16[4,1280,80]{1,2,0:T(8,128)(2,1)} %param.6) | copy-start | bytes 2457604

commit v4 on v3

v4 whole, which is shorter than its diff:
```python
import functools

import jax
import jax.numpy as jnp
from jax import lax
from jax.experimental import pallas as pl
from jax.experimental.pallas import tpu as pltpu
from jax.sharding import Mesh, PartitionSpec as P

Y, Z, X, C = 4, 16, 4, 2
ZL = 2
ZH = Z // ZL
EXTRA = 128
BF = jnp.bfloat16
F32 = jnp.float32
NEAR = ("y", "zl", "x", "c")


def slot_kernel(groups, rows_hbm, router_hbm, pieces_ref, combine_ref, rows, router_in, sems):
    count, depth = rows_hbm.shape
    width = depth // ZL
    first = pltpu.make_async_copy(router_hbm, router_in, sems.at[0])
    second = pltpu.make_async_copy(rows_hbm, rows, sems.at[1])
    first.start()
    second.start()
    first.wait()

    slots = router_in.shape[0]
    row = lax.broadcasted_iota(jnp.int32, (slots, slots), 0)
    column = lax.broadcasted_iota(jnp.int32, (slots, slots), 1)
    chosen = (column == (row % groups) * Y + row // groups).astype(F32).astype(BF)
    router = jnp.dot(chosen, router_in[...], preferred_element_type=F32).astype(BF)
    second.wait()
    values = lax.dot_general(router, rows[...], (((1,), (1,)), ((), ())), preferred_element_type=F32)
    top = jnp.max(values, axis=1, keepdims=True)
    weights = jnp.exp(values - top)
    total = jnp.sum(weights, axis=1, keepdims=True)
    summed = jnp.dot(weights.astype(BF), rows[...], preferred_element_type=F32)
    mean = summed / total
    lse = top + jnp.log(total)
    high = lse.astype(BF).astype(F32)
    mid = (lse - high).astype(BF).astype(F32)
    low = lse - high - mid
    lane = lax.broadcasted_iota(jnp.int32, (slots, EXTRA), 1)
    tail = jnp.where(lane == 0, high, jnp.where(lane == 1, mid, jnp.where(lane == 2, low, 0.0)))
    size = groups * ZL
    for y in range(Y):
        block = mean[y * groups : (y + 1) * groups]
        halves = [block[:, z * width : (z + 1) * width] for z in range(ZL)]
        pieces_ref[y * size : (y + 1) * size, :width] = jnp.concatenate(halves, axis=0).astype(BF)
        end = tail[y * groups : (y + 1) * groups]
        pieces_ref[y * size : (y + 1) * size, width:] = jnp.concatenate([end] * ZL, axis=0).astype(BF)

    combine = jnp.exp(values - jnp.max(values, axis=0, keepdims=True))
    combine_ref[...] = (combine / jnp.sum(combine, axis=0, keepdims=True)).astype(BF)


def in_hbm(array):
    return pltpu.with_memory_space_constraint(array, pltpu.HBM)


def slot_sums(rows, router, groups):
    count, depth = rows.shape
    slots = router.shape[1]
    width = depth // ZL
    return pl.pallas_call(
        functools.partial(slot_kernel, groups),
        out_shape=(
            jax.ShapeDtypeStruct((slots * ZL, width + EXTRA), BF),
            jax.ShapeDtypeStruct((slots, count), BF),
        ),
        in_specs=[pl.BlockSpec(memory_space=pltpu.HBM), pl.BlockSpec(memory_space=pltpu.HBM)],
        out_specs=(pl.BlockSpec(memory_space=pltpu.VMEM), pl.BlockSpec(memory_space=pltpu.VMEM)),
        scratch_shapes=[
            pltpu.VMEM((count, depth), BF),
            pltpu.VMEM((slots, depth), BF),
            pltpu.SemaphoreType.DMA((2,)),
        ],
        compiler_params=pltpu.CompilerParams(vmem_limit_bytes=32 * 1024 * 1024),
        name="slot_sums",
    )(in_hbm(rows), in_hbm(router.T))


def exact_parts(v):
    high = lax.reduce_precision(v, 8, 7)
    rest = v - high
    mid = lax.reduce_precision(rest, 8, 7)
    low = rest - mid
    return jnp.stack([high, mid, low], axis=-1).astype(BF)


def packed(mean, lse):
    tail = jnp.pad(exact_parts(lse), [(0, 0)] * lse.ndim + [(0, EXTRA - 3)])
    return jnp.concatenate([mean.astype(BF), tail], axis=-1)


def merged(pieces, width):
    mean = pieces[..., :width].astype(F32)
    lse = jnp.sum(pieces[..., width : width + 3].astype(F32), axis=-1)
    top = jnp.max(lse, axis=0)
    weight = jnp.exp(lse - top)
    total = jnp.sum(weight, axis=0)
    mean = jnp.sum(mean * weight[..., None], axis=0) / total[..., None]
    return mean, top + jnp.log(total)


def scatter(pieces):
    count, width = pieces.shape
    got = lax.all_to_all(pieces.reshape(count, 2, width // 2), NEAR, 0, 0, tiled=True)
    return got.reshape(Y * ZL, count // (Y * ZL), width)


def spread(block, axes, count):
    copies = jnp.broadcast_to(block[None], (count,) + block.shape)
    return lax.all_to_all(copies, axes, 0, 0, tiled=True)


def on_device(patches, router, w_in, w_out):
    own = w_in.shape[0]
    slots = router.shape[1]
    groups = slots // own
    depth = patches.shape[2]
    width = depth // ZL

    pieces, combine = slot_sums(patches[0], router, groups)
    mean, lse = merged(scatter(pieces), width)
    got = spread(packed(mean, lse), "zh", ZH)
    mean, _ = merged(got, width)
    got = spread(mean.astype(BF), ("y", "zl"), Y * ZL)
    slot_in = got.reshape(Y, ZL, groups, width).transpose(2, 0, 1, 3).reshape(groups, own, depth)

    hidden = jax.nn.gelu(jnp.einsum("bed,edf->bef", slot_in, w_in, preferred_element_type=F32)).astype(BF)
    partial_out = jnp.einsum("bef,efd->bed", hidden, w_out, preferred_element_type=F32).astype(BF)

    pieces = partial_out.reshape(groups, Y, ZL, width).transpose(1, 2, 0, 3).reshape(Y * ZL * groups, width)
    total = jnp.sum(scatter(pieces).astype(F32), axis=0).astype(BF)
    got = spread(total, "zh", ZH)
    total = jnp.sum(got.astype(F32), axis=0).astype(BF)
    got = spread(total, ("y", "zl"), Y * ZL)
    slot_out = got.reshape(Y, ZL, groups, width).transpose(0, 2, 1, 3).reshape(slots, depth)

    mixed = lax.dot_general(combine, slot_out, (((0,), (0,)), ((), ())), preferred_element_type=F32)
    return mixed.astype(BF)[None]


def solution(mesh):
    fine = Mesh(mesh.devices.reshape(Y, ZH, ZL, X, C), ("y", "zh", "zl", "x", "c"))
    ctx, exp = ("y", "zh", "zl"), ("x", "c")
    placed = (P(exp, ctx, None), P(), P(exp, None, ctx), P(exp, ctx, None))
    return jax.shard_map(
        on_device, mesh=fine, in_specs=placed, out_specs=P(exp, ctx, None), check_vma=False
    )
```

time: 102 us -> 98.6 us (0.967)
  local copies, waits for them, and re-layouts: 3.14 us -> 0.64 us
  Pallas kernels: 0 us -> 2.37 us
  matrix products: 3.96 us -> 2.06 us
  other arithmetic: 2.15 us -> 0.57 us
    pallas_call x0 -> x1, Pallas kernels: none -> 2.37 us  [slot_sums(): pl.pallas_call(functools.partial(slot_kernel, groups), out_shape=(jax.Sha...]
    dot_general x3 -> x1, matrix products: 3.48 us -> 1.58 us  [on_device(): lax.dot_general(combine, slot_out, (((0,), (0,)), ((), ())), preferred_el...]
    unnamed x14 -> x6, local copies, waits for them, and re-layouts: 1.97 us -> 0.24 us
    all_to_all x2 -> x0, other arithmetic: 1.34 us -> none  [the longest x1 0.68 us: on_device(): lax.all_to_all(pieces.reshape(Y * ZL * groups, width), NEAR, 0, 0, tiled=...]
where the time goes in v4:
time: 98.6 us; the launch traced here: 97.5 us
  blocking collectives  91.8 us (93%)
  Pallas kernels  2.37 us (2%)
  matrix products  2.06 us (2%)
    all_to_all x4, blocking collectives, spread(): return lax.all_to_all(copies, axes, 0, 0, tiled=True)  63.6 us
    all_to_all x2, blocking collectives, scatter(): lax.all_to_all(pieces.reshape(count, 2, width // 2), NEAR, 0, 0, tiled=True)  28.2 us
    pallas_call x1, Pallas kernels, slot_sums(): pl.pallas_call(functools.partial(slot_kernel, groups), out_shape=(jax.Sha...  2.37 us

profile of v4, /device:TPU:6, one launch (start us, length us, event | category | flops | bytes accessed | tf_op | source)
XLA Modules:
  0.0 97.5 jit_solution(1729711798643715409)
XLA Ops:
  0.0 0.0 copy-start
  0.0 0.0 copy-start.1
  0.0 2.4 %slot_sums.1 = (bf16[64,768]{1,0:T(8,128)(2,1)S(1)}, bf16[32,512]{1,0:T(8,128)(2,1)S(1)}) custom-call(bf16[512,1280]{1,0:T(8,128)(2,1)} %bitcast.41, bf16[32,1280]{1,0:T(8,128)(2,1)} %bitcast.45), custom_call_target="tpu_custom_call" | custom-call | tf_op jit(solution)/shard_map/slot_sums/pallas_call | solution.py:66
  2.4 15.9 %all_to_all.30 = bf16[64,2,384]{2,1,0:T(2,128)(2,1)S(1)} all-to-all(bf16[64,2,384]{2,1,0:T(2,128)(2,1)S(1)} %reshape.117), channel_id=1, replica_groups=mesh['y'=4,'zh'=8,'zl'=2,'x'=4,'c'=2] {'y','zl','x','c'}, dimensions={0} | all-to-all | bytes 196608 | tf_op jit(solution)/shard_map/all_to_all | solution.py:109
  18.3 0.1 reshape.118
  18.4 0.1 convert_reduce_fusion
  18.5 0.1 multiply_reduce_fusion.1
  18.6 0.1 divide_convert_fusion.1
  18.7 0.1 copy.13
  18.8 28.5 %all_to_all.31 = bf16[8,8,768]{2,1,0:T(8,128)(2,1)S(1)} all-to-all(bf16[8,8,768]{2,1,0:T(8,128)(2,1)S(1)} %broadcast_in_dim.10), channel_id=1, replica_groups=mesh['y'=4,'zh'=8,'zl'=2,'x'=4,'c'=2] {'zh'}, dimensions={0} | all-to-all | bytes 196608 | tf_op jit(solution)/shard_map/all_to_all | solution.py:115
  47.3 0.1 copy.12
  47.5 0.1 multiply_reduce_fusion
  47.6 0.1 divide_convert_fusion
  47.7 9.4 %all_to_all.32 = bf16[8,8,640]{2,1,0:T(8,128)(2,1)S(1)} all-to-all(bf16[8,8,640]{2,1,0:T(8,128)(2,1)S(1)} %broadcast_in_dim.11), channel_id=1, replica_groups=mesh['y'=4,'zh'=8,'zl'=2,'x'=4,'c'=2] {'y','zl'}, dimensions={0} | all-to-all | bytes 163840 | tf_op jit(solution)/shard_map/all_to_all | solution.py:115
  57.1 0.0 copy-done
  57.1 0.0 copy-done.1
  57.1 0.5 convolution_convert_fusion.1
  57.6 0.1 reshape_reshape.3
  57.7 12.3 %all_to_all.33 = bf16[64,2,320]{2,1,0:T(2,128)(2,1)S(1)} all-to-all(bf16[64,2,320]{2,1,0:T(2,128)(2,1)S(1)} %reshape_reshape.3), channel_id=1, replica_groups=mesh['y'=4,'zh'=8,'zl'=2,'x'=4,'c'=2] {'y','zl','x','c'}, dimensions={0} | all-to-all | bytes 163840 | tf_op jit(solution)/shard_map/all_to_all | solution.py:109
  70.1 0.1 reshape.122
  70.2 16.9 %all_to_all.34 = bf16[8,8,640]{2,1,0:T(8,128)(2,1)S(1)} all-to-all(bf16[8,8,640]{2,1,0:T(8,128)(2,1)S(1)} %broadcast_in_dim.12), channel_id=1, replica_groups=mesh['y'=4,'zh'=8,'zl'=2,'x'=4,'c'=2] {'zh'}, dimensions={0} | all-to-all | bytes 163840 | tf_op jit(solution)/shard_map/all_to_all | solution.py:115
  87.1 8.8 %all_to_all.35 = bf16[8,8,640]{2,1,0:T(8,128)(2,1)S(1)} all-to-all(bf16[8,8,640]{2,1,0:T(8,128)(2,1)S(1)} %broadcast_in_dim.13), channel_id=1, replica_groups=mesh['y'=4,'zh'=8,'zl'=2,'x'=4,'c'=2] {'y','zl'}, dimensions={0} | all-to-all | bytes 163840 | tf_op jit(solution)/shard_map/all_to_all | solution.py:115
  95.9 1.6 %fusion = bf16[1,512,1280]{2,1,0:T(8,128)(2,1)} fusion(bf16[32,512]{1,0:T(8,128)(2,1)S(1)} %get-tuple-element.7, bf16[32,1280]{1,0:T(8,128)(2,1)S(1)} %bitcast.44), kind=kOutput, calls=%fused_computation.1 | convolution fusion | flops 42598400 | bytes 1425408 | tf_op jit(solution)/shard_map/dot_general | solution.py:142
  (16 shorter events, 0.2 us)
Async XLA Ops:
  0.0 57.1 %copy-start = (bf16[4,80,1280]{2,1,0:T(8,128)(2,1)S(1)}, bf16[4,80,1280]{2,1,0:T(8,128)(2,1)}, u32[]{:S(2)}) copy-start(bf16[4,80,1280]{2,1,0:T(8,128)(2,1)} %param.7) | copy-start | bytes 2457604
  0.0 57.1 %copy-start.1 = (bf16[4,1280,80]{1,2,0:T(8,128)(2,1)S(1)}, bf16[4,1280,80]{1,2,0:T(8,128)(2,1)}, u32[]{:S(2)}) copy-start(bf16[4,1280,80]{1,2,0:T(8,128)(2,1)} %param.6) | copy-start | bytes 2457604

commit v5 on v4

--- a/solution.py
+++ b/solution.py
@@ -110,9 +110,10 @@
     return got.reshape(Y * ZL, count // (Y * ZL), width)
 
 
-def spread(block, axes, count):
+def spread(block, axes, count, first=0):
     copies = jnp.broadcast_to(block[None], (count,) + block.shape)
-    return lax.all_to_all(copies, axes, 0, 0, tiled=True)
+    order = [[(first + i) % count for i in range(count)]] if first else None
+    return lax.all_to_all(copies, axes, 0, 0, tiled=True, axis_index_groups=order)
 
 
 def on_device(patches, router, w_in, w_out):
@@ -124,7 +125,7 @@
 
     pieces, combine = slot_sums(patches[0], router, groups)
     mean, lse = merged(scatter(pieces), width)
-    got = spread(packed(mean, lse), "zh", ZH)
+    got = spread(packed(mean, lse), "zh", ZH, ZH // 2)
     mean, _ = merged(got, width)
     got = spread(mean.astype(BF), ("y", "zl"), Y * ZL)
     slot_in = got.reshape(Y, ZL, groups, width).transpose(2, 0, 1, 3).reshape(groups, own, depth)

time: 98.6 us -> 101 us (1.024)
  blocking collectives: 91.8 us -> 93.8 us
    all_to_all x4, blocking collectives: 63.6 us -> 65.5 us  [spread(): lax.all_to_all(copies, axes, 0, 0, tiled=True, axis_index_groups=order)]
where the time goes in v5:
time: 101 us; the launch traced here: 99.6 us
  blocking collectives  93.8 us (93%)
  Pallas kernels  2.37 us (2%)
  matrix products  2.06 us (2%)
    all_to_all x4, blocking collectives, spread(): lax.all_to_all(copies, axes, 0, 0, tiled=True, axis_index_groups=order)  65.5 us
    all_to_all x2, blocking collectives, scatter(): lax.all_to_all(pieces.reshape(count, 2, width // 2), NEAR, 0, 0, tiled=True)  28.3 us
    pallas_call x1, Pallas kernels, slot_sums(): pl.pallas_call(functools.partial(slot_kernel, groups), out_shape=(jax.Sha...  2.37 us

profile of v5, /device:TPU:6, one launch (start us, length us, event | category | flops | bytes accessed | tf_op | source)
XLA Modules:
  0.0 99.6 jit_solution(8614430740265048330)
XLA Ops:
  0.0 0.0 copy-start
  0.0 0.0 copy-start.1
  0.0 2.4 %slot_sums.1 = (bf16[64,768]{1,0:T(8,128)(2,1)S(1)}, bf16[32,512]{1,0:T(8,128)(2,1)S(1)}) custom-call(bf16[512,1280]{1,0:T(8,128)(2,1)} %bitcast.41, bf16[32,1280]{1,0:T(8,128)(2,1)} %bitcast.45), custom_call_target="tpu_custom_call" | custom-call | tf_op jit(solution)/shard_map/slot_sums/pallas_call | solution.py:66
  2.4 15.9 %all_to_all.30 = bf16[64,2,384]{2,1,0:T(2,128)(2,1)S(1)} all-to-all(bf16[64,2,384]{2,1,0:T(2,128)(2,1)S(1)} %reshape.117), channel_id=1, replica_groups=mesh['y'=4,'zh'=8,'zl'=2,'x'=4,'c'=2] {'y','zl','x','c'}, dimensions={0} | all-to-all | bytes 196608 | tf_op jit(solution)/shard_map/all_to_all | solution.py:109
  18.3 0.1 reshape.118
  18.4 0.1 convert_reduce_fusion
  18.5 0.1 multiply_reduce_fusion.1
  18.6 0.1 divide_convert_fusion.1
  18.7 0.1 copy.13
  18.8 21.7 %all_to_all.31 = bf16[8,8,768]{2,1,0:T(8,128)(2,1)S(1)} all-to-all(bf16[8,8,768]{2,1,0:T(8,128)(2,1)S(1)} %broadcast_in_dim.10), channel_id=1, replica_groups={{64,80,96,112,0,16,32,48},{65,81,97,113,1,17,33,49},{66,82,98,114,2,18,..., dimensions={0} | all-to-all | bytes 196608 | tf_op jit(solution)/shard_map/all_to_all | solution.py:116
  40.5 0.1 copy.12
  40.7 0.1 multiply_reduce_fusion
  40.8 0.1 divide_convert_fusion
  40.9 9.6 %all_to_all.32 = bf16[8,8,640]{2,1,0:T(8,128)(2,1)S(1)} all-to-all(bf16[8,8,640]{2,1,0:T(8,128)(2,1)S(1)} %broadcast_in_dim.11), channel_id=1, replica_groups=mesh['y'=4,'zh'=8,'zl'=2,'x'=4,'c'=2] {'y','zl'}, dimensions={0} | all-to-all | bytes 163840 | tf_op jit(solution)/shard_map/all_to_all | solution.py:116
  50.5 0.0 copy-done
  50.5 0.0 copy-done.1
  50.5 0.5 convolution_convert_fusion.1
  50.9 0.1 reshape_reshape.3
  51.1 12.5 %all_to_all.33 = bf16[64,2,320]{2,1,0:T(2,128)(2,1)S(1)} all-to-all(bf16[64,2,320]{2,1,0:T(2,128)(2,1)S(1)} %reshape_reshape.3), channel_id=1, replica_groups=mesh['y'=4,'zh'=8,'zl'=2,'x'=4,'c'=2] {'y','zl','x','c'}, dimensions={0} | all-to-all | bytes 163840 | tf_op jit(solution)/shard_map/all_to_all | solution.py:109
  63.6 0.1 reshape.122
  63.7 24.9 %all_to_all.34 = bf16[8,8,640]{2,1,0:T(8,128)(2,1)S(1)} all-to-all(bf16[8,8,640]{2,1,0:T(8,128)(2,1)S(1)} %broadcast_in_dim.12), channel_id=1, replica_groups=mesh['y'=4,'zh'=8,'zl'=2,'x'=4,'c'=2] {'zh'}, dimensions={0} | all-to-all | bytes 163840 | tf_op jit(solution)/shard_map/all_to_all | solution.py:116
  88.7 9.3 %all_to_all.35 = bf16[8,8,640]{2,1,0:T(8,128)(2,1)S(1)} all-to-all(bf16[8,8,640]{2,1,0:T(8,128)(2,1)S(1)} %broadcast_in_dim.13), channel_id=1, replica_groups=mesh['y'=4,'zh'=8,'zl'=2,'x'=4,'c'=2] {'y','zl'}, dimensions={0} | all-to-all | bytes 163840 | tf_op jit(solution)/shard_map/all_to_all | solution.py:116
  98.0 1.6 %fusion = bf16[1,512,1280]{2,1,0:T(8,128)(2,1)} fusion(bf16[32,512]{1,0:T(8,128)(2,1)S(1)} %get-tuple-element.7, bf16[32,1280]{1,0:T(8,128)(2,1)S(1)} %bitcast.44), kind=kOutput, calls=%fused_computation.1 | convolution fusion | flops 42598400 | bytes 1425408 | tf_op jit(solution)/shard_map/dot_general | solution.py:143
  (16 shorter events, 0.2 us)
Async XLA Ops:
  0.0 50.5 %copy-start = (bf16[4,80,1280]{2,1,0:T(8,128)(2,1)S(1)}, bf16[4,80,1280]{2,1,0:T(8,128)(2,1)}, u32[]{:S(2)}) copy-start(bf16[4,80,1280]{2,1,0:T(8,128)(2,1)} %param.7) | copy-start | bytes 2457604
  0.0 50.5 %copy-start.1 = (bf16[4,1280,80]{1,2,0:T(8,128)(2,1)S(1)}, bf16[4,1280,80]{1,2,0:T(8,128)(2,1)}, u32[]{:S(2)}) copy-start(bf16[4,1280,80]{1,2,0:T(8,128)(2,1)} %param.6) | copy-start | bytes 2457604

commit v6 on v5

--- a/solution.py
+++ b/solution.py
@@ -135,7 +135,7 @@
 
     pieces = partial_out.reshape(groups, Y, ZL, width).transpose(1, 2, 0, 3).reshape(Y * ZL * groups, width)
     total = jnp.sum(scatter(pieces).astype(F32), axis=0).astype(BF)
-    got = spread(total, "zh", ZH)
+    got = spread(total, "zh", ZH, ZH // 2)
     total = jnp.sum(got.astype(F32), axis=0).astype(BF)
     got = spread(total, ("y", "zl"), Y * ZL)
     slot_out = got.reshape(Y, ZL, groups, width).transpose(0, 2, 1, 3).reshape(slots, depth)

time: 101 us -> 92.3 us (0.914)
  blocking collectives: 93.8 us -> 85.5 us
    all_to_all x4, blocking collectives: 65.5 us -> 57.2 us  [spread(): lax.all_to_all(copies, axes, 0, 0, tiled=True, axis_index_groups=order)]
where the time goes in v6:
time: 92.3 us; the launch traced here: 91.2 us
  blocking collectives  85.5 us (93%)
  Pallas kernels  2.37 us (3%)
  matrix products  2.06 us (2%)
    all_to_all x4, blocking collectives, spread(): lax.all_to_all(copies, axes, 0, 0, tiled=True, axis_index_groups=order)  57.2 us
    all_to_all x2, blocking collectives, scatter(): lax.all_to_all(pieces.reshape(count, 2, width // 2), NEAR, 0, 0, tiled=True)  28.3 us
    pallas_call x1, Pallas kernels, slot_sums(): pl.pallas_call(functools.partial(slot_kernel, groups), out_shape=(jax.Sha...  2.37 us

profile of v6, /device:TPU:6, one launch (start us, length us, event | category | flops | bytes accessed | tf_op | source)
XLA Modules:
  0.0 91.2 jit_solution(17614966142233605289)
XLA Ops:
  0.0 0.0 copy-start
  0.0 0.0 copy-start.1
  0.0 2.4 %slot_sums.1 = (bf16[64,768]{1,0:T(8,128)(2,1)S(1)}, bf16[32,512]{1,0:T(8,128)(2,1)S(1)}) custom-call(bf16[512,1280]{1,0:T(8,128)(2,1)} %bitcast.41, bf16[32,1280]{1,0:T(8,128)(2,1)} %bitcast.45), custom_call_target="tpu_custom_call" | custom-call | tf_op jit(solution)/shard_map/slot_sums/pallas_call | solution.py:66
  2.4 15.9 %all_to_all.30 = bf16[64,2,384]{2,1,0:T(2,128)(2,1)S(1)} all-to-all(bf16[64,2,384]{2,1,0:T(2,128)(2,1)S(1)} %reshape.117), channel_id=1, replica_groups=mesh['y'=4,'zh'=8,'zl'=2,'x'=4,'c'=2] {'y','zl','x','c'}, dimensions={0} | all-to-all | bytes 196608 | tf_op jit(solution)/shard_map/all_to_all | solution.py:109
  18.3 0.1 reshape.118
  18.4 0.1 convert_reduce_fusion
  18.5 0.1 multiply_reduce_fusion.1
  18.6 0.1 divide_convert_fusion.1
  18.7 0.1 copy.13
  18.8 21.7 %all_to_all.31 = bf16[8,8,768]{2,1,0:T(8,128)(2,1)S(1)} all-to-all(bf16[8,8,768]{2,1,0:T(8,128)(2,1)S(1)} %broadcast_in_dim.10), channel_id=1, replica_groups={{64,80,96,112,0,16,32,48},{65,81,97,113,1,17,33,49},{66,82,98,114,2,18,..., dimensions={0} | all-to-all | bytes 196608 | tf_op jit(solution)/shard_map/all_to_all | solution.py:116
  40.5 0.1 copy.12
  40.7 0.1 multiply_reduce_fusion
  40.8 0.1 divide_convert_fusion
  40.9 9.6 %all_to_all.32 = bf16[8,8,640]{2,1,0:T(8,128)(2,1)S(1)} all-to-all(bf16[8,8,640]{2,1,0:T(8,128)(2,1)S(1)} %broadcast_in_dim.11), channel_id=1, replica_groups=mesh['y'=4,'zh'=8,'zl'=2,'x'=4,'c'=2] {'y','zl'}, dimensions={0} | all-to-all | bytes 163840 | tf_op jit(solution)/shard_map/all_to_all | solution.py:116
  50.5 0.0 copy-done
  50.5 0.0 copy-done.1
  50.5 0.5 convolution_convert_fusion.1
  50.9 0.1 reshape_reshape.3
  51.1 12.5 %all_to_all.33 = bf16[64,2,320]{2,1,0:T(2,128)(2,1)S(1)} all-to-all(bf16[64,2,320]{2,1,0:T(2,128)(2,1)S(1)} %reshape_reshape.3), channel_id=1, replica_groups=mesh['y'=4,'zh'=8,'zl'=2,'x'=4,'c'=2] {'y','zl','x','c'}, dimensions={0} | all-to-all | bytes 163840 | tf_op jit(solution)/shard_map/all_to_all | solution.py:109
  63.6 0.1 reshape.122
  63.7 16.3 %all_to_all.34 = bf16[8,8,640]{2,1,0:T(8,128)(2,1)S(1)} all-to-all(bf16[8,8,640]{2,1,0:T(8,128)(2,1)S(1)} %broadcast_in_dim.12), channel_id=1, replica_groups={{64,80,96,112,0,16,32,48},{65,81,97,113,1,17,33,49},{66,82,98,114,2,18,..., dimensions={0} | all-to-all | bytes 163840 | tf_op jit(solution)/shard_map/all_to_all | solution.py:116
  80.1 9.6 %all_to_all.35 = bf16[8,8,640]{2,1,0:T(8,128)(2,1)S(1)} all-to-all(bf16[8,8,640]{2,1,0:T(8,128)(2,1)S(1)} %broadcast_in_dim.13), channel_id=1, replica_groups=mesh['y'=4,'zh'=8,'zl'=2,'x'=4,'c'=2] {'y','zl'}, dimensions={0} | all-to-all | bytes 163840 | tf_op jit(solution)/shard_map/all_to_all | solution.py:116
  89.6 1.6 %fusion = bf16[1,512,1280]{2,1,0:T(8,128)(2,1)} fusion(bf16[32,512]{1,0:T(8,128)(2,1)S(1)} %get-tuple-element.7, bf16[32,1280]{1,0:T(8,128)(2,1)S(1)} %bitcast.44), kind=kOutput, calls=%fused_computation.1 | convolution fusion | flops 42598400 | bytes 1425408 | tf_op jit(solution)/shard_map/dot_general | solution.py:143
  (16 shorter events, 0.2 us)
Async XLA Ops:
  0.0 50.5 %copy-start = (bf16[4,80,1280]{2,1,0:T(8,128)(2,1)S(1)}, bf16[4,80,1280]{2,1,0:T(8,128)(2,1)}, u32[]{:S(2)}) copy-start(bf16[4,80,1280]{2,1,0:T(8,128)(2,1)} %param.7) | copy-start | bytes 2457604
  0.0 50.5 %copy-start.1 = (bf16[4,1280,80]{1,2,0:T(8,128)(2,1)S(1)}, bf16[4,1280,80]{1,2,0:T(8,128)(2,1)}, u32[]{:S(2)}) copy-start(bf16[4,1280,80]{1,2,0:T(8,128)(2,1)} %param.6) | copy-start | bytes 2457604

commit v7 on v6

--- a/solution.py
+++ b/solution.py
@@ -14,6 +14,14 @@
 BF = jnp.bfloat16
 F32 = jnp.float32
 NEAR = ("y", "zl", "x", "c")
+Y0, X0, H0 = 2, 2, ZH // 2
+
+
+def rolled(*dims):
+    members = [0]
+    for size, first in dims:
+        members = [m * size + (first + i) % size for m in members for i in range(size)]
+    return [members]
 
 
 def slot_kernel(groups, rows_hbm, router_hbm, pieces_ref, combine_ref, rows, router_in, sems):
@@ -28,7 +36,7 @@
     slots = router_in.shape[0]
     row = lax.broadcasted_iota(jnp.int32, (slots, slots), 0)
     column = lax.broadcasted_iota(jnp.int32, (slots, slots), 1)
-    chosen = (column == (row % groups) * Y + row // groups).astype(F32).astype(BF)
+    chosen = (column == ((row + X0 * C) % groups) * Y + (row // groups + Y0) % Y).astype(F32).astype(BF)
     router = jnp.dot(chosen, router_in[...], preferred_element_type=F32).astype(BF)
     second.wait()
     values = lax.dot_general(router, rows[...], (((1,), (1,)), ((), ())), preferred_element_type=F32)
@@ -104,15 +112,16 @@
     return mean, top + jnp.log(total)
 
 
-def scatter(pieces):
+def scatter(pieces, y0):
     count, width = pieces.shape
-    got = lax.all_to_all(pieces.reshape(count, 2, width // 2), NEAR, 0, 0, tiled=True)
+    order = rolled((Y, y0), (ZL, 0), (X, X0), (C, 0))
+    pieces = pieces.reshape(count, 2, width // 2)
+    got = lax.all_to_all(pieces, NEAR, 0, 0, tiled=True, axis_index_groups=order)
     return got.reshape(Y * ZL, count // (Y * ZL), width)
 
 
-def spread(block, axes, count, first=0):
-    copies = jnp.broadcast_to(block[None], (count,) + block.shape)
-    order = [[(first + i) % count for i in range(count)]] if first else None
+def spread(block, axes, order):
+    copies = jnp.broadcast_to(block[None], (len(order[0]),) + block.shape)
     return lax.all_to_all(copies, axes, 0, 0, tiled=True, axis_index_groups=order)
 
 
@@ -124,20 +133,20 @@
     width = depth // ZL
 
     pieces, combine = slot_sums(patches[0], router, groups)
-    mean, lse = merged(scatter(pieces), width)
-    got = spread(packed(mean, lse), "zh", ZH, ZH // 2)
+    mean, lse = merged(scatter(pieces, Y0), width)
+    got = spread(packed(mean, lse), "zh", rolled((ZH, H0)))
     mean, _ = merged(got, width)
-    got = spread(mean.astype(BF), ("y", "zl"), Y * ZL)
+    got = spread(mean.astype(BF), ("y", "zl"), rolled((Y, 0), (ZL, 0)))
     slot_in = got.reshape(Y, ZL, groups, width).transpose(2, 0, 1, 3).reshape(groups, own, depth)
 
     hidden = jax.nn.gelu(jnp.einsum("bed,edf->bef", slot_in, w_in, preferred_element_type=F32)).astype(BF)
     partial_out = jnp.einsum("bef,efd->bed", hidden, w_out, preferred_element_type=F32).astype(BF)
 
     pieces = partial_out.reshape(groups, Y, ZL, width).transpose(1, 2, 0, 3).reshape(Y * ZL * groups, width)
-    total = jnp.sum(scatter(pieces).astype(F32), axis=0).astype(BF)
-    got = spread(total, "zh", ZH, ZH // 2)
+    total = jnp.sum(scatter(pieces, 0).astype(F32), axis=0).astype(BF)
+    got = spread(total, "zh", rolled((ZH, H0)))
     total = jnp.sum(got.astype(F32), axis=0).astype(BF)
-    got = spread(total, ("y", "zl"), Y * ZL)
+    got = spread(total, ("y", "zl"), rolled((Y, Y0), (ZL, 0)))
     slot_out = got.reshape(Y, ZL, groups, width).transpose(0, 2, 1, 3).reshape(slots, depth)
 
     mixed = lax.dot_general(combine, slot_out, (((0,), (0,)), ((), ())), preferred_element_type=F32)

time: 92.3 us -> 90.7 us (0.983)
  blocking collectives: 85.5 us -> 84.1 us
    all_to_all x4, blocking collectives: 57.2 us -> 55.5 us  [spread(): lax.all_to_all(copies, axes, 0, 0, tiled=True, axis_index_groups=order)]
where the time goes in v7:
time: 90.7 us; the launch traced here: 89.8 us
  blocking collectives  84.1 us (93%)
  Pallas kernels  2.37 us (3%)
  matrix products  2.06 us (2%)
    all_to_all x4, blocking collectives, spread(): lax.all_to_all(copies, axes, 0, 0, tiled=True, axis_index_groups=order)  55.5 us
    all_to_all x2, blocking collectives, scatter(): lax.all_to_all(pieces, NEAR, 0, 0, tiled=True, axis_index_groups=order)  28.6 us
    pallas_call x1, Pallas kernels, slot_sums(): pl.pallas_call(functools.partial(slot_kernel, groups), out_shape=(jax.Sha...  2.37 us

profile of v7, /device:TPU:6, one launch (start us, length us, event | category | flops | bytes accessed | tf_op | source)
XLA Modules:
  0.0 89.8 jit_solution(2937053174030017677)
XLA Ops:
  0.0 0.0 copy-start
  0.0 0.0 copy-start.1
  0.0 2.4 %slot_sums.1 = (bf16[64,768]{1,0:T(8,128)(2,1)S(1)}, bf16[32,512]{1,0:T(8,128)(2,1)S(1)}) custom-call(bf16[512,1280]{1,0:T(8,128)(2,1)} %bitcast.41, bf16[32,1280]{1,0:T(8,128)(2,1)} %bitcast.45), custom_call_target="tpu_custom_call" | custom-call | tf_op jit(solution)/shard_map/slot_sums/pallas_call | solution.py:74
  2.4 16.3 %all_to_all.30 = bf16[64,2,384]{2,1,0:T(2,128)(2,1)S(1)} all-to-all(bf16[64,2,384]{2,1,0:T(2,128)(2,1)S(1)} %reshape.117), channel_id=1, replica_groups={{260,261,262,263,256,257,258,259,268,269,270,271,264,265,266,267,388,38..., dimensions={0} | all-to-all | bytes 196608 | tf_op jit(solution)/shard_map/all_to_all | solution.py:119
  18.7 0.1 reshape.118
  18.8 0.1 convert_reduce_fusion
  18.9 0.1 multiply_reduce_fusion.1
  19.0 0.1 divide_convert_fusion.1
  19.1 0.1 copy.13
  19.2 19.3 %all_to_all.31 = bf16[8,8,768]{2,1,0:T(8,128)(2,1)S(1)} all-to-all(bf16[8,8,768]{2,1,0:T(8,128)(2,1)S(1)} %broadcast_in_dim.10), channel_id=1, replica_groups={{64,80,96,112,0,16,32,48},{65,81,97,113,1,17,33,49},{66,82,98,114,2,18,..., dimensions={0} | all-to-all | bytes 196608 | tf_op jit(solution)/shard_map/all_to_all | solution.py:125
  38.5 0.1 copy.12
  38.7 0.1 multiply_reduce_fusion
  38.8 0.1 divide_convert_fusion
  38.9 11.1 %all_to_all.32 = bf16[8,8,640]{2,1,0:T(8,128)(2,1)S(1)} all-to-all(bf16[8,8,640]{2,1,0:T(8,128)(2,1)S(1)} %broadcast_in_dim.11), channel_id=1, replica_groups={{0,8,128,136,256,264,384,392},{1,9,129,137,257,265,385,393},{2,10,130,1..., dimensions={0} | all-to-all | bytes 163840 | tf_op jit(solution)/shard_map/all_to_all | solution.py:125
  50.0 0.0 copy-done
  50.0 0.0 copy-done.1
  50.0 0.5 convolution_convert_fusion.1
  50.5 0.1 reshape_reshape.3
  50.7 12.3 %all_to_all.33 = bf16[64,2,320]{2,1,0:T(2,128)(2,1)S(1)} all-to-all(bf16[64,2,320]{2,1,0:T(2,128)(2,1)S(1)} %reshape_reshape.3), channel_id=1, replica_groups={{4,5,6,7,0,1,2,3,12,13,14,15,8,9,10,11,132,133,134,135,128,129,130,131,..., dimensions={0} | all-to-all | bytes 163840 | tf_op jit(solution)/shard_map/all_to_all | solution.py:119
  63.0 0.1 reshape.122
  63.1 16.6 %all_to_all.34 = bf16[8,8,640]{2,1,0:T(8,128)(2,1)S(1)} all-to-all(bf16[8,8,640]{2,1,0:T(8,128)(2,1)S(1)} %broadcast_in_dim.12), channel_id=1, replica_groups={{64,80,96,112,0,16,32,48},{65,81,97,113,1,17,33,49},{66,82,98,114,2,18,..., dimensions={0} | all-to-all | bytes 163840 | tf_op jit(solution)/shard_map/all_to_all | solution.py:125
  79.8 8.4 %all_to_all.35 = bf16[8,8,640]{2,1,0:T(8,128)(2,1)S(1)} all-to-all(bf16[8,8,640]{2,1,0:T(8,128)(2,1)S(1)} %broadcast_in_dim.13), channel_id=1, replica_groups={{256,264,384,392,0,8,128,136},{257,265,385,393,1,9,129,137},{258,266,38..., dimensions={0} | all-to-all | bytes 163840 | tf_op jit(solution)/shard_map/all_to_all | solution.py:125
  88.3 1.6 %fusion = bf16[1,512,1280]{2,1,0:T(8,128)(2,1)} fusion(bf16[32,512]{1,0:T(8,128)(2,1)S(1)} %get-tuple-element.7, bf16[32,1280]{1,0:T(8,128)(2,1)S(1)} %bitcast.44), kind=kOutput, calls=%fused_computation.1 | convolution fusion | flops 42598400 | bytes 1425408 | tf_op jit(solution)/shard_map/dot_general | solution.py:152
  (16 shorter events, 0.2 us)
Async XLA Ops:
  0.0 50.0 %copy-start = (bf16[4,80,1280]{2,1,0:T(8,128)(2,1)S(1)}, bf16[4,80,1280]{2,1,0:T(8,128)(2,1)}, u32[]{:S(2)}) copy-start(bf16[4,80,1280]{2,1,0:T(8,128)(2,1)} %param.7) | copy-start | bytes 2457604
  0.0 50.0 %copy-start.1 = (bf16[4,1280,80]{1,2,0:T(8,128)(2,1)S(1)}, bf16[4,1280,80]{1,2,0:T(8,128)(2,1)}, u32[]{:S(2)}) copy-start(bf16[4,1280,80]{1,2,0:T(8,128)(2,1)} %param.6) | copy-start | bytes 2457604

commit v8 on v7

--- a/solution.py
+++ b/solution.py
@@ -36,7 +36,7 @@
     slots = router_in.shape[0]
     row = lax.broadcasted_iota(jnp.int32, (slots, slots), 0)
     column = lax.broadcasted_iota(jnp.int32, (slots, slots), 1)
-    chosen = (column == ((row + X0 * C) % groups) * Y + (row // groups + Y0) % Y).astype(F32).astype(BF)
+    chosen = (column == ((row + X0 * C) % groups) * Y + row // groups).astype(F32).astype(BF)
     router = jnp.dot(chosen, router_in[...], preferred_element_type=F32).astype(BF)
     second.wait()
     values = lax.dot_general(router, rows[...], (((1,), (1,)), ((), ())), preferred_element_type=F32)
@@ -112,9 +112,9 @@
     return mean, top + jnp.log(total)
 
 
-def scatter(pieces, y0):
+def scatter(pieces):
     count, width = pieces.shape
-    order = rolled((Y, y0), (ZL, 0), (X, X0), (C, 0))
+    order = rolled((Y, Y0), (ZL, 0), (X, X0), (C, 0))
     pieces = pieces.reshape(count, 2, width // 2)
     got = lax.all_to_all(pieces, NEAR, 0, 0, tiled=True, axis_index_groups=order)
     return got.reshape(Y * ZL, count // (Y * ZL), width)
@@ -133,17 +133,17 @@
     width = depth // ZL
 
     pieces, combine = slot_sums(patches[0], router, groups)
-    mean, lse = merged(scatter(pieces, Y0), width)
+    mean, lse = merged(scatter(pieces), width)
     got = spread(packed(mean, lse), "zh", rolled((ZH, H0)))
     mean, _ = merged(got, width)
-    got = spread(mean.astype(BF), ("y", "zl"), rolled((Y, 0), (ZL, 0)))
+    got = spread(mean.astype(BF), ("y", "zl"), rolled((Y, Y0), (ZL, 0)))
     slot_in = got.reshape(Y, ZL, groups, width).transpose(2, 0, 1, 3).reshape(groups, own, depth)
 
     hidden = jax.nn.gelu(jnp.einsum("bed,edf->bef", slot_in, w_in, preferred_element_type=F32)).astype(BF)
     partial_out = jnp.einsum("bef,efd->bed", hidden, w_out, preferred_element_type=F32).astype(BF)
 
     pieces = partial_out.reshape(groups, Y, ZL, width).transpose(1, 2, 0, 3).reshape(Y * ZL * groups, width)
-    total = jnp.sum(scatter(pieces, 0).astype(F32), axis=0).astype(BF)
+    total = jnp.sum(scatter(pieces).astype(F32), axis=0).astype(BF)
     got = spread(total, "zh", rolled((ZH, H0)))
     total = jnp.sum(got.astype(F32), axis=0).astype(BF)
     got = spread(total, ("y", "zl"), rolled((Y, Y0), (ZL, 0)))

time: 90.7 us -> 89.7 us (0.989)
  no operation moved by 1% of the time
where the time goes in v8:
time: 89.7 us; the launch traced here: 89.3 us
  blocking collectives  83.5 us (93%)
  Pallas kernels  2.37 us (3%)
  matrix products  2.06 us (2%)
    all_to_all x4, blocking collectives, spread(): lax.all_to_all(copies, axes, 0, 0, tiled=True, axis_index_groups=order)  55.2 us
    all_to_all x2, blocking collectives, scatter(): lax.all_to_all(pieces, NEAR, 0, 0, tiled=True, axis_index_groups=order)  28.4 us
    pallas_call x1, Pallas kernels, slot_sums(): pl.pallas_call(functools.partial(slot_kernel, groups), out_shape=(jax.Sha...  2.37 us

profile of v8, /device:TPU:6, one launch (start us, length us, event | category | flops | bytes accessed | tf_op | source)
XLA Modules:
  0.0 89.3 jit_solution(3210688939078402390)
XLA Ops:
  0.0 0.0 copy-start
  0.0 0.0 copy-start.1
  0.0 2.4 %slot_sums.1 = (bf16[64,768]{1,0:T(8,128)(2,1)S(1)}, bf16[32,512]{1,0:T(8,128)(2,1)S(1)}) custom-call(bf16[512,1280]{1,0:T(8,128)(2,1)} %bitcast.41, bf16[32,1280]{1,0:T(8,128)(2,1)} %bitcast.45), custom_call_target="tpu_custom_call" | custom-call | tf_op jit(solution)/shard_map/slot_sums/pallas_call | solution.py:74
  2.4 16.3 %all_to_all.30 = bf16[64,2,384]{2,1,0:T(2,128)(2,1)S(1)} all-to-all(bf16[64,2,384]{2,1,0:T(2,128)(2,1)S(1)} %reshape.117), channel_id=1, replica_groups={{260,261,262,263,256,257,258,259,268,269,270,271,264,265,266,267,388,38..., dimensions={0} | all-to-all | bytes 196608 | tf_op jit(solution)/shard_map/all_to_all | solution.py:119
  18.7 0.1 reshape.118
  18.8 0.1 convert_reduce_fusion
  18.9 0.1 multiply_reduce_fusion.1
  19.0 0.1 divide_convert_fusion.1
  19.1 0.1 copy.13
  19.2 19.3 %all_to_all.31 = bf16[8,8,768]{2,1,0:T(8,128)(2,1)S(1)} all-to-all(bf16[8,8,768]{2,1,0:T(8,128)(2,1)S(1)} %broadcast_in_dim.10), channel_id=1, replica_groups={{64,80,96,112,0,16,32,48},{65,81,97,113,1,17,33,49},{66,82,98,114,2,18,..., dimensions={0} | all-to-all | bytes 196608 | tf_op jit(solution)/shard_map/all_to_all | solution.py:125
  38.5 0.1 copy.12
  38.7 0.1 multiply_reduce_fusion
  38.8 0.1 divide_convert_fusion
  38.9 9.8 %all_to_all.32 = bf16[8,8,640]{2,1,0:T(8,128)(2,1)S(1)} all-to-all(bf16[8,8,640]{2,1,0:T(8,128)(2,1)S(1)} %broadcast_in_dim.11), channel_id=1, replica_groups={{256,264,384,392,0,8,128,136},{257,265,385,393,1,9,129,137},{258,266,38..., dimensions={0} | all-to-all | bytes 163840 | tf_op jit(solution)/shard_map/all_to_all | solution.py:125
  48.7 0.0 copy-done
  48.7 0.0 copy-done.1
  48.7 0.5 convolution_convert_fusion.1
  49.2 0.1 reshape_reshape.3
  49.3 12.1 %all_to_all.33 = bf16[64,2,320]{2,1,0:T(2,128)(2,1)S(1)} all-to-all(bf16[64,2,320]{2,1,0:T(2,128)(2,1)S(1)} %reshape_reshape.3), channel_id=1, replica_groups={{260,261,262,263,256,257,258,259,268,269,270,271,264,265,266,267,388,38..., dimensions={0} | all-to-all | bytes 163840 | tf_op jit(solution)/shard_map/all_to_all | solution.py:119
  61.4 0.1 reshape.122
  61.6 16.2 %all_to_all.34 = bf16[8,8,640]{2,1,0:T(8,128)(2,1)S(1)} all-to-all(bf16[8,8,640]{2,1,0:T(8,128)(2,1)S(1)} %broadcast_in_dim.12), channel_id=1, replica_groups={{64,80,96,112,0,16,32,48},{65,81,97,113,1,17,33,49},{66,82,98,114,2,18,..., dimensions={0} | all-to-all | bytes 163840 | tf_op jit(solution)/shard_map/all_to_all | solution.py:125
  77.9 9.8 %all_to_all.35 = bf16[8,8,640]{2,1,0:T(8,128)(2,1)S(1)} all-to-all(bf16[8,8,640]{2,1,0:T(8,128)(2,1)S(1)} %broadcast_in_dim.13), channel_id=1, replica_groups={{256,264,384,392,0,8,128,136},{257,265,385,393,1,9,129,137},{258,266,38..., dimensions={0} | all-to-all | bytes 163840 | tf_op jit(solution)/shard_map/all_to_all | solution.py:125
  87.7 1.6 %fusion = bf16[1,512,1280]{2,1,0:T(8,128)(2,1)} fusion(bf16[32,512]{1,0:T(8,128)(2,1)S(1)} %get-tuple-element.7, bf16[32,1280]{1,0:T(8,128)(2,1)S(1)} %bitcast.44), kind=kOutput, calls=%fused_computation.1 | convolution fusion | flops 42598400 | bytes 1425408 | tf_op jit(solution)/shard_map/dot_general | solution.py:152
  (16 shorter events, 0.2 us)
Async XLA Ops:
  0.0 48.7 %copy-start = (bf16[4,80,1280]{2,1,0:T(8,128)(2,1)S(1)}, bf16[4,80,1280]{2,1,0:T(8,128)(2,1)}, u32[]{:S(2)}) copy-start(bf16[4,80,1280]{2,1,0:T(8,128)(2,1)} %param.7) | copy-start | bytes 2457604
  0.0 48.7 %copy-start.1 = (bf16[4,1280,80]{1,2,0:T(8,128)(2,1)S(1)}, bf16[4,1280,80]{1,2,0:T(8,128)(2,1)}, u32[]{:S(2)}) copy-start(bf16[4,1280,80]{1,2,0:T(8,128)(2,1)} %param.6) | copy-start | bytes 2457604

commit v9 on v8

--- a/solution.py
+++ b/solution.py
@@ -14,7 +14,7 @@
 BF = jnp.bfloat16
 F32 = jnp.float32
 NEAR = ("y", "zl", "x", "c")
-Y0, X0, H0 = 2, 2, ZH // 2
+Y0, X0, H0 = 3, 3, 5
 
 
 def rolled(*dims):

time: 89.7 us -> 89.5 us (level)
  no operation moved by 1% of the time
where the time goes in v9:
time: 89.5 us; the launch traced here: 89.1 us
  blocking collectives  83.4 us (93%)
  Pallas kernels  2.37 us (3%)
  matrix products  2.06 us (2%)
    all_to_all x4, blocking collectives, spread(): lax.all_to_all(copies, axes, 0, 0, tiled=True, axis_index_groups=order)  54.3 us
    all_to_all x2, blocking collectives, scatter(): lax.all_to_all(pieces, NEAR, 0, 0, tiled=True, axis_index_groups=order)  29.1 us
    pallas_call x1, Pallas kernels, slot_sums(): pl.pallas_call(functools.partial(slot_kernel, groups), out_shape=(jax.Sha...  2.37 us

profile of v9, /device:TPU:6, one launch (start us, length us, event | category | flops | bytes accessed | tf_op | source)
XLA Modules:
  0.0 89.1 jit_solution(1015811908143603005)
XLA Ops:
  0.0 0.0 copy-start
  0.0 0.0 copy-start.1
  0.0 2.4 %slot_sums.1 = (bf16[64,768]{1,0:T(8,128)(2,1)S(1)}, bf16[32,512]{1,0:T(8,128)(2,1)S(1)}) custom-call(bf16[512,1280]{1,0:T(8,128)(2,1)} %bitcast.41, bf16[32,1280]{1,0:T(8,128)(2,1)} %bitcast.45), custom_call_target="tpu_custom_call" | custom-call | tf_op jit(solution)/shard_map/slot_sums/pallas_call | solution.py:74
  2.4 16.6 %all_to_all.30 = bf16[64,2,384]{2,1,0:T(2,128)(2,1)S(1)} all-to-all(bf16[64,2,384]{2,1,0:T(2,128)(2,1)S(1)} %reshape.117), channel_id=1, replica_groups={{390,391,384,385,386,387,388,389,398,399,392,393,394,395,396,397,6,7,0,..., dimensions={0} | all-to-all | bytes 196608 | tf_op jit(solution)/shard_map/all_to_all | solution.py:119
  19.0 0.1 reshape.118
  19.1 0.1 convert_reduce_fusion
  19.2 0.1 multiply_reduce_fusion.1
  19.3 0.1 divide_convert_fusion.1
  19.4 0.1 copy.13
  19.6 20.4 %all_to_all.31 = bf16[8,8,768]{2,1,0:T(8,128)(2,1)S(1)} all-to-all(bf16[8,8,768]{2,1,0:T(8,128)(2,1)S(1)} %broadcast_in_dim.10), channel_id=1, replica_groups={{80,96,112,0,16,32,48,64},{81,97,113,1,17,33,49,65},{82,98,114,2,18,34,..., dimensions={0} | all-to-all | bytes 196608 | tf_op jit(solution)/shard_map/all_to_all | solution.py:125
  40.0 0.1 copy.12
  40.2 0.1 multiply_reduce_fusion
  40.3 0.1 divide_convert_fusion
  40.4 8.7 %all_to_all.32 = bf16[8,8,640]{2,1,0:T(8,128)(2,1)S(1)} all-to-all(bf16[8,8,640]{2,1,0:T(8,128)(2,1)S(1)} %broadcast_in_dim.11), channel_id=1, replica_groups={{384,392,0,8,128,136,256,264},{385,393,1,9,129,137,257,265},{386,394,2,..., dimensions={0} | all-to-all | bytes 163840 | tf_op jit(solution)/shard_map/all_to_all | solution.py:125
  49.0 0.0 copy-done
  49.0 0.0 copy-done.1
  49.0 0.5 convolution_convert_fusion.1
  49.5 0.1 reshape_reshape.3
  49.7 12.4 %all_to_all.33 = bf16[64,2,320]{2,1,0:T(2,128)(2,1)S(1)} all-to-all(bf16[64,2,320]{2,1,0:T(2,128)(2,1)S(1)} %reshape_reshape.3), channel_id=1, replica_groups={{390,391,384,385,386,387,388,389,398,399,392,393,394,395,396,397,6,7,0,..., dimensions={0} | all-to-all | bytes 163840 | tf_op jit(solution)/shard_map/all_to_all | solution.py:119
  62.1 0.1 reshape.122
  62.3 16.5 %all_to_all.34 = bf16[8,8,640]{2,1,0:T(8,128)(2,1)S(1)} all-to-all(bf16[8,8,640]{2,1,0:T(8,128)(2,1)S(1)} %broadcast_in_dim.12), channel_id=1, replica_groups={{80,96,112,0,16,32,48,64},{81,97,113,1,17,33,49,65},{82,98,114,2,18,34,..., dimensions={0} | all-to-all | bytes 163840 | tf_op jit(solution)/shard_map/all_to_all | solution.py:125
  78.8 8.7 %all_to_all.35 = bf16[8,8,640]{2,1,0:T(8,128)(2,1)S(1)} all-to-all(bf16[8,8,640]{2,1,0:T(8,128)(2,1)S(1)} %broadcast_in_dim.13), channel_id=1, replica_groups={{384,392,0,8,128,136,256,264},{385,393,1,9,129,137,257,265},{386,394,2,..., dimensions={0} | all-to-all | bytes 163840 | tf_op jit(solution)/shard_map/all_to_all | solution.py:125
  87.5 1.6 %fusion = bf16[1,512,1280]{2,1,0:T(8,128)(2,1)} fusion(bf16[32,512]{1,0:T(8,128)(2,1)S(1)} %get-tuple-element.7, bf16[32,1280]{1,0:T(8,128)(2,1)S(1)} %bitcast.44), kind=kOutput, calls=%fused_computation.1 | convolution fusion | flops 42598400 | bytes 1425408 | tf_op jit(solution)/shard_map/dot_general | solution.py:152
  (16 shorter events, 0.2 us)
Async XLA Ops:
  0.0 49.0 %copy-start = (bf16[4,80,1280]{2,1,0:T(8,128)(2,1)S(1)}, bf16[4,80,1280]{2,1,0:T(8,128)(2,1)}, u32[]{:S(2)}) copy-start(bf16[4,80,1280]{2,1,0:T(8,128)(2,1)} %param.7) | copy-start | bytes 2457604
  0.0 49.0 %copy-start.1 = (bf16[4,1280,80]{1,2,0:T(8,128)(2,1)S(1)}, bf16[4,1280,80]{1,2,0:T(8,128)(2,1)}, u32[]{:S(2)}) copy-start(bf16[4,1280,80]{1,2,0:T(8,128)(2,1)} %param.6) | copy-start | bytes 2457604

commit v10 on v9

--- a/solution.py
+++ b/solution.py
@@ -14,7 +14,8 @@
 BF = jnp.bfloat16
 F32 = jnp.float32
 NEAR = ("y", "zl", "x", "c")
-Y0, X0, H0 = 3, 3, 5
+Y0, X0 = 3, 3
+LONG_IN, LONG_OUT = [[5, 4, 6, 3, 7, 2, 0, 1]], [[5, 0, 1, 2, 7, 3, 6, 4]]
 
 
 def rolled(*dims):
@@ -134,7 +135,7 @@
 
     pieces, combine = slot_sums(patches[0], router, groups)
     mean, lse = merged(scatter(pieces), width)
-    got = spread(packed(mean, lse), "zh", rolled((ZH, H0)))
+    got = spread(packed(mean, lse), "zh", LONG_IN)
     mean, _ = merged(got, width)
     got = spread(mean.astype(BF), ("y", "zl"), rolled((Y, Y0), (ZL, 0)))
     slot_in = got.reshape(Y, ZL, groups, width).transpose(2, 0, 1, 3).reshape(groups, own, depth)
@@ -144,7 +145,7 @@
 
     pieces = partial_out.reshape(groups, Y, ZL, width).transpose(1, 2, 0, 3).reshape(Y * ZL * groups, width)
     total = jnp.sum(scatter(pieces).astype(F32), axis=0).astype(BF)
-    got = spread(total, "zh", rolled((ZH, H0)))
+    got = spread(total, "zh", LONG_OUT)
     total = jnp.sum(got.astype(F32), axis=0).astype(BF)
     got = spread(total, ("y", "zl"), rolled((Y, Y0), (ZL, 0)))
     slot_out = got.reshape(Y, ZL, groups, width).transpose(0, 2, 1, 3).reshape(slots, depth)

time: 89.5 us -> 90.4 us (1.010)
    all_to_all x4, blocking collectives: 54.3 us -> 55.4 us  [spread(): lax.all_to_all(copies, axes, 0, 0, tiled=True, axis_index_groups=order)]
where the time goes in v10:
time: 90.4 us; the launch traced here: 90.1 us
  blocking collectives  84.3 us (93%)
  Pallas kernels  2.37 us (3%)
  matrix products  2.06 us (2%)
    all_to_all x4, blocking collectives, spread(): lax.all_to_all(copies, axes, 0, 0, tiled=True, axis_index_groups=order)  55.4 us
    all_to_all x2, blocking collectives, scatter(): lax.all_to_all(pieces, NEAR, 0, 0, tiled=True, axis_index_groups=order)  28.9 us
    pallas_call x1, Pallas kernels, slot_sums(): pl.pallas_call(functools.partial(slot_kernel, groups), out_shape=(jax.Sha...  2.37 us

profile of v10, /device:TPU:6, one launch (start us, length us, event | category | flops | bytes accessed | tf_op | source)
XLA Modules:
  0.0 90.1 jit_solution(2533142165677403617)
XLA Ops:
  0.0 0.0 copy-start
  0.0 0.0 copy-start.1
  0.0 2.4 %slot_sums.1 = (bf16[64,768]{1,0:T(8,128)(2,1)S(1)}, bf16[32,512]{1,0:T(8,128)(2,1)S(1)}) custom-call(bf16[512,1280]{1,0:T(8,128)(2,1)} %bitcast.41, bf16[32,1280]{1,0:T(8,128)(2,1)} %bitcast.45), custom_call_target="tpu_custom_call" | custom-call | tf_op jit(solution)/shard_map/slot_sums/pallas_call | solution.py:75
  2.4 16.6 %all_to_all.30 = bf16[64,2,384]{2,1,0:T(2,128)(2,1)S(1)} all-to-all(bf16[64,2,384]{2,1,0:T(2,128)(2,1)S(1)} %reshape.117), channel_id=1, replica_groups={{390,391,384,385,386,387,388,389,398,399,392,393,394,395,396,397,6,7,0,..., dimensions={0} | all-to-all | bytes 196608 | tf_op jit(solution)/shard_map/all_to_all | solution.py:120
  19.0 0.1 reshape.118
  19.1 0.1 convert_reduce_fusion
  19.2 0.1 multiply_reduce_fusion.1
  19.3 0.1 divide_convert_fusion.1
  19.4 0.1 copy.13
  19.6 20.6 %all_to_all.31 = bf16[8,8,768]{2,1,0:T(8,128)(2,1)S(1)} all-to-all(bf16[8,8,768]{2,1,0:T(8,128)(2,1)S(1)} %broadcast_in_dim.10), channel_id=1, replica_groups={{80,64,96,48,112,32,0,16},{81,65,97,49,113,33,1,17},{82,66,98,50,114,34..., dimensions={0} | all-to-all | bytes 196608 | tf_op jit(solution)/shard_map/all_to_all | solution.py:126
  40.1 0.1 copy.12
  40.3 0.1 multiply_reduce_fusion
  40.4 0.1 divide_convert_fusion
  40.5 8.7 %all_to_all.32 = bf16[8,8,640]{2,1,0:T(8,128)(2,1)S(1)} all-to-all(bf16[8,8,640]{2,1,0:T(8,128)(2,1)S(1)} %broadcast_in_dim.11), channel_id=1, replica_groups={{384,392,0,8,128,136,256,264},{385,393,1,9,129,137,257,265},{386,394,2,..., dimensions={0} | all-to-all | bytes 163840 | tf_op jit(solution)/shard_map/all_to_all | solution.py:126
  49.2 0.0 copy-done
  49.2 0.0 copy-done.1
  49.2 0.5 convolution_convert_fusion.1
  49.7 0.1 reshape_reshape.3
  49.8 12.3 %all_to_all.33 = bf16[64,2,320]{2,1,0:T(2,128)(2,1)S(1)} all-to-all(bf16[64,2,320]{2,1,0:T(2,128)(2,1)S(1)} %reshape_reshape.3), channel_id=1, replica_groups={{390,391,384,385,386,387,388,389,398,399,392,393,394,395,396,397,6,7,0,..., dimensions={0} | all-to-all | bytes 163840 | tf_op jit(solution)/shard_map/all_to_all | solution.py:120
  62.1 0.1 reshape.122
  62.3 17.3 %all_to_all.34 = bf16[8,8,640]{2,1,0:T(8,128)(2,1)S(1)} all-to-all(bf16[8,8,640]{2,1,0:T(8,128)(2,1)S(1)} %broadcast_in_dim.12), channel_id=1, replica_groups={{80,0,16,32,112,48,96,64},{81,1,17,33,113,49,97,65},{82,2,18,34,114,50,..., dimensions={0} | all-to-all | bytes 163840 | tf_op jit(solution)/shard_map/all_to_all | solution.py:126
  79.6 8.8 %all_to_all.35 = bf16[8,8,640]{2,1,0:T(8,128)(2,1)S(1)} all-to-all(bf16[8,8,640]{2,1,0:T(8,128)(2,1)S(1)} %broadcast_in_dim.13), channel_id=1, replica_groups={{384,392,0,8,128,136,256,264},{385,393,1,9,129,137,257,265},{386,394,2,..., dimensions={0} | all-to-all | bytes 163840 | tf_op jit(solution)/shard_map/all_to_all | solution.py:126
  88.5 1.6 %fusion = bf16[1,512,1280]{2,1,0:T(8,128)(2,1)} fusion(bf16[32,512]{1,0:T(8,128)(2,1)S(1)} %get-tuple-element.7, bf16[32,1280]{1,0:T(8,128)(2,1)S(1)} %bitcast.44), kind=kOutput, calls=%fused_computation.1 | convolution fusion | flops 42598400 | bytes 1425408 | tf_op jit(solution)/shard_map/dot_general | solution.py:153
  (16 shorter events, 0.2 us)
Async XLA Ops:
  0.0 49.2 %copy-start = (bf16[4,80,1280]{2,1,0:T(8,128)(2,1)S(1)}, bf16[4,80,1280]{2,1,0:T(8,128)(2,1)}, u32[]{:S(2)}) copy-start(bf16[4,80,1280]{2,1,0:T(8,128)(2,1)} %param.7) | copy-start | bytes 2457604
  0.0 49.2 %copy-start.1 = (bf16[4,1280,80]{1,2,0:T(8,128)(2,1)S(1)}, bf16[4,1280,80]{1,2,0:T(8,128)(2,1)}, u32[]{:S(2)}) copy-start(bf16[4,1280,80]{1,2,0:T(8,128)(2,1)} %param.6) | copy-start | bytes 2457604

commit v11 on v9

--- a/solution.py
+++ b/solution.py
@@ -14,7 +14,8 @@
 BF = jnp.bfloat16
 F32 = jnp.float32
 NEAR = ("y", "zl", "x", "c")
-Y0, X0, H0 = 3, 3, 5
+Y0, X0, C0, H0 = 3, 3, 1, 5
+ROWS = 128
 
 
 def rolled(*dims):
@@ -36,7 +37,8 @@
     slots = router_in.shape[0]
     row = lax.broadcasted_iota(jnp.int32, (slots, slots), 0)
     column = lax.broadcasted_iota(jnp.int32, (slots, slots), 1)
-    chosen = (column == ((row + X0 * C) % groups) * Y + row // groups).astype(F32).astype(BF)
+    owner = (row + X0 * C) % groups // C * C + (row + C0) % C
+    chosen = (column == owner * Y + row // groups).astype(F32).astype(BF)
     router = jnp.dot(chosen, router_in[...], preferred_element_type=F32).astype(BF)
     second.wait()
     values = lax.dot_general(router, rows[...], (((1,), (1,)), ((), ())), preferred_element_type=F32)
@@ -89,6 +91,32 @@
     )(in_hbm(rows), in_hbm(router.T))
 
 
+def mix_kernel(combine_ref, slots_ref, mixed_hbm, mixed, sems):
+    copies = []
+    for i in range(mixed.shape[0] // ROWS):
+        part = pl.ds(i * ROWS, ROWS)
+        mixed[part] = lax.dot_general(
+            combine_ref[:, part], slots_ref[...], (((0,), (0,)), ((), ())), preferred_element_type=F32
+        ).astype(BF)
+        copies.append(pltpu.make_async_copy(mixed.at[part], mixed_hbm.at[part], sems.at[i]))
+        copies[-1].start()
+    for copy in copies:
+        copy.wait()
+
+
+def mix(combine, slot_out):
+    count, depth = combine.shape[1], slot_out.shape[1]
+    return pl.pallas_call(
+        mix_kernel,
+        out_shape=jax.ShapeDtypeStruct((count, depth), BF),
+        in_specs=[pl.BlockSpec(memory_space=pltpu.VMEM), pl.BlockSpec(memory_space=pltpu.VMEM)],
+        out_specs=pl.BlockSpec(memory_space=pl.ANY),
+        scratch_shapes=[pltpu.VMEM((count, depth), BF), pltpu.SemaphoreType.DMA((count // ROWS,))],
+        compiler_params=pltpu.CompilerParams(vmem_limit_bytes=32 * 1024 * 1024),
+        name="mix",
+    )(combine, slot_out)
+
+
 def exact_parts(v):
     high = lax.reduce_precision(v, 8, 7)
     rest = v - high
@@ -114,7 +142,7 @@
 
 def scatter(pieces):
     count, width = pieces.shape
-    order = rolled((Y, Y0), (ZL, 0), (X, X0), (C, 0))
+    order = rolled((Y, Y0), (ZL, 0), (X, X0), (C, C0))
     pieces = pieces.reshape(count, 2, width // 2)
     got = lax.all_to_all(pieces, NEAR, 0, 0, tiled=True, axis_index_groups=order)
     return got.reshape(Y * ZL, count // (Y * ZL), width)
@@ -149,8 +177,7 @@
     got = spread(total, ("y", "zl"), rolled((Y, Y0), (ZL, 0)))
     slot_out = got.reshape(Y, ZL, groups, width).transpose(0, 2, 1, 3).reshape(slots, depth)
 
-    mixed = lax.dot_general(combine, slot_out, (((0,), (0,)), ((), ())), preferred_element_type=F32)
-    return mixed.astype(BF)[None]
+    return mix(combine, slot_out)[None]
 
 
 def solution(mesh):

time: 89.5 us -> 89.3 us (level)
  matrix products: 2.06 us -> 0.48 us
  Pallas kernels: 2.37 us -> 3.74 us
    dot_general x1 -> x0, matrix products: 1.58 us -> none  [on_device(): lax.dot_general(combine, slot_out, (((0,), (0,)), ((), ())), preferred_el...]
    pallas_call x0 -> x1, Pallas kernels: none -> 1.37 us  [mix(): pl.pallas_call(mix_kernel, out_shape=jax.ShapeDtypeStruct((count, depth),...]
where the time goes in v11:
time: 89.3 us; the launch traced here: 89 us
  blocking collectives  83.5 us (94%)
  Pallas kernels  3.74 us (4%)
    all_to_all x4, blocking collectives, spread(): lax.all_to_all(copies, axes, 0, 0, tiled=True, axis_index_groups=order)  55.2 us
    all_to_all x2, blocking collectives, scatter(): lax.all_to_all(pieces, NEAR, 0, 0, tiled=True, axis_index_groups=order)  28.3 us
    pallas_call x1, Pallas kernels, slot_sums(): pl.pallas_call(functools.partial(slot_kernel, groups), out_shape=(jax.Sha...  2.37 us

profile of v11, /device:TPU:6, one launch (start us, length us, event | category | flops | bytes accessed | tf_op | source)
XLA Modules:
  0.0 89.0 jit_solution(9953102109657214908)
XLA Ops:
  0.0 0.0 copy-start
  0.0 0.0 copy-start.1
  0.0 2.4 %slot_sums.1 = (bf16[64,768]{1,0:T(8,128)(2,1)S(1)}, bf16[32,512]{1,0:T(8,128)(2,1)S(1)}) custom-call(bf16[512,1280]{1,0:T(8,128)(2,1)} %bitcast.39, bf16[32,1280]{1,0:T(8,128)(2,1)} %bitcast.42), custom_call_target="tpu_custom_call" | custom-call | tf_op jit(solution)/shard_map/slot_sums/pallas_call | solution.py:76
  2.4 16.4 %all_to_all.30 = bf16[64,2,384]{2,1,0:T(2,128)(2,1)S(1)} all-to-all(bf16[64,2,384]{2,1,0:T(2,128)(2,1)S(1)} %reshape.117), channel_id=1, replica_groups={{391,390,385,384,387,386,389,388,399,398,393,392,395,394,397,396,7,6,1,..., dimensions={0} | all-to-all | bytes 196608 | tf_op jit(solution)/shard_map/all_to_all | solution.py:147
  18.8 0.1 reshape.118
  18.9 0.1 convert_reduce_fusion
  19.0 0.1 multiply_reduce_fusion.1
  19.1 0.1 divide_convert_fusion.1
  19.2 0.1 copy.13
  19.3 20.5 %all_to_all.31 = bf16[8,8,768]{2,1,0:T(8,128)(2,1)S(1)} all-to-all(bf16[8,8,768]{2,1,0:T(8,128)(2,1)S(1)} %broadcast_in_dim.10), channel_id=1, replica_groups={{80,96,112,0,16,32,48,64},{81,97,113,1,17,33,49,65},{82,98,114,2,18,34,..., dimensions={0} | all-to-all | bytes 196608 | tf_op jit(solution)/shard_map/all_to_all | solution.py:153
  39.9 0.1 copy.12
  40.1 0.1 multiply_reduce_fusion
  40.1 0.1 divide_convert_fusion
  40.2 8.7 %all_to_all.32 = bf16[8,8,640]{2,1,0:T(8,128)(2,1)S(1)} all-to-all(bf16[8,8,640]{2,1,0:T(8,128)(2,1)S(1)} %broadcast_in_dim.11), channel_id=1, replica_groups={{384,392,0,8,128,136,256,264},{385,393,1,9,129,137,257,265},{386,394,2,..., dimensions={0} | all-to-all | bytes 163840 | tf_op jit(solution)/shard_map/all_to_all | solution.py:153
  48.9 0.0 copy-done
  48.9 0.0 copy-done.1
  48.9 0.5 convolution_convert_fusion
  49.4 0.1 reshape_reshape.3
  49.5 11.9 %all_to_all.33 = bf16[64,2,320]{2,1,0:T(2,128)(2,1)S(1)} all-to-all(bf16[64,2,320]{2,1,0:T(2,128)(2,1)S(1)} %reshape_reshape.3), channel_id=1, replica_groups={{391,390,385,384,387,386,389,388,399,398,393,392,395,394,397,396,7,6,1,..., dimensions={0} | all-to-all | bytes 163840 | tf_op jit(solution)/shard_map/all_to_all | solution.py:147
  61.5 0.1 reshape.122
  61.6 17.3 %all_to_all.34 = bf16[8,8,640]{2,1,0:T(8,128)(2,1)S(1)} all-to-all(bf16[8,8,640]{2,1,0:T(8,128)(2,1)S(1)} %broadcast_in_dim.12), channel_id=1, replica_groups={{80,96,112,0,16,32,48,64},{81,97,113,1,17,33,49,65},{82,98,114,2,18,34,..., dimensions={0} | all-to-all | bytes 163840 | tf_op jit(solution)/shard_map/all_to_all | solution.py:153
  78.9 8.7 %all_to_all.35 = bf16[8,8,640]{2,1,0:T(8,128)(2,1)S(1)} all-to-all(bf16[8,8,640]{2,1,0:T(8,128)(2,1)S(1)} %broadcast_in_dim.13), channel_id=1, replica_groups={{384,392,0,8,128,136,256,264},{385,393,1,9,129,137,257,265},{386,394,2,..., dimensions={0} | all-to-all | bytes 163840 | tf_op jit(solution)/shard_map/all_to_all | solution.py:153
  87.6 1.4 %mix.1 = bf16[512,1280]{1,0:T(8,128)(2,1)} custom-call(bf16[32,512]{1,0:T(8,128)(2,1)S(1)} %get-tuple-element.7.combine_ref, bf16[32,1280]{1,0:T(8,128)(2,1)S(1)} %bitcast.38), custom_call_target="tpu_custom_call" | custom-call | tf_op jit(solution)/shard_map/mix/pallas_call | solution.py:109
  (16 shorter events, 0.2 us)
Async XLA Ops:
  0.0 48.9 %copy-start = (bf16[4,80,1280]{2,1,0:T(8,128)(2,1)S(1)}, bf16[4,80,1280]{2,1,0:T(8,128)(2,1)}, u32[]{:S(2)}) copy-start(bf16[4,80,1280]{2,1,0:T(8,128)(2,1)} %param.7) | copy-start | bytes 2457604
  0.0 48.9 %copy-start.1 = (bf16[4,1280,80]{1,2,0:T(8,128)(2,1)S(1)}, bf16[4,1280,80]{1,2,0:T(8,128)(2,1)}, u32[]{:S(2)}) copy-start(bf16[4,1280,80]{1,2,0:T(8,128)(2,1)} %param.6) | copy-start | bytes 2457604

commit v12 on v11

--- a/solution.py
+++ b/solution.py
@@ -9,20 +9,49 @@
 
 Y, Z, X, C = 4, 16, 4, 2
 ZL = 2
-ZH = Z // ZL
 EXTRA = 128
+ROWS = 128
 BF = jnp.bfloat16
 F32 = jnp.float32
-NEAR = ("y", "zl", "x", "c")
-Y0, X0, C0, H0 = 3, 3, 1, 5
-ROWS = 128
-
-
-def rolled(*dims):
-    members = [0]
-    for size, first in dims:
-        members = [m * size + (first + i) % size for m in members for i in range(size)]
-    return [members]
+AXES = ("y", "z", "x", "c")
+Y0, X0, C0 = 3, 3, 1
+HALVES = ((0, 2, 4, 6, 9, 11, 13, 15), (1, 3, 5, 7, 8, 10, 12, 14))
+LONG_IN, LONG_OUT = (11, 10), (9, 10)
+
+
+def member(y, z, x, c):
+    return ((y % Y * Z + z) * X + x % X) * C + c % C
+
+
+def near_groups():
+    return [
+        [
+            member(Y0 + y, half[k], X0 + x, C0 + c)
+            for y in range(Y)
+            for half in HALVES
+            for x in range(X)
+            for c in range(C)
+        ]
+        for k in range(Z // ZL)
+    ]
+
+
+def gather_groups():
+    return [
+        [member(Y0 + y, half[k], x, c) for y in range(Y) for half in HALVES]
+        for k in range(Z // ZL)
+        for x in range(X)
+        for c in range(C)
+    ]
+
+
+def long_groups(starts):
+    groups = []
+    for half, start in zip(HALVES, starts):
+        first = half.index(start)
+        planes = half[first:] + half[:first]
+        groups += [[member(y, z, x, c) for z in planes] for y in range(Y) for x in range(X) for c in range(C)]
+    return groups
 
 
 def slot_kernel(groups, rows_hbm, router_hbm, pieces_ref, combine_ref, rows, router_in, sems):
@@ -140,17 +169,18 @@
     return mean, top + jnp.log(total)
 
 
+def exchange(pieces, groups):
+    return lax.all_to_all(pieces, AXES, 0, 0, tiled=True, axis_index_groups=groups)
+
+
 def scatter(pieces):
     count, width = pieces.shape
-    order = rolled((Y, Y0), (ZL, 0), (X, X0), (C, C0))
-    pieces = pieces.reshape(count, 2, width // 2)
-    got = lax.all_to_all(pieces, NEAR, 0, 0, tiled=True, axis_index_groups=order)
+    got = exchange(pieces.reshape(count, 2, width // 2), near_groups())
     return got.reshape(Y * ZL, count // (Y * ZL), width)
 
 
-def spread(block, axes, order):
-    copies = jnp.broadcast_to(block[None], (len(order[0]),) + block.shape)
-    return lax.all_to_all(copies, axes, 0, 0, tiled=True, axis_index_groups=order)
+def spread(block, groups):
+    return exchange(jnp.broadcast_to(block[None], (len(groups[0]),) + block.shape), groups)
 
 
 def on_device(patches, router, w_in, w_out):
@@ -162,9 +192,9 @@
 
     pieces, combine = slot_sums(patches[0], router, groups)
     mean, lse = merged(scatter(pieces), width)
-    got = spread(packed(mean, lse), "zh", rolled((ZH, H0)))
+    got = spread(packed(mean, lse), long_groups(LONG_IN))
     mean, _ = merged(got, width)
-    got = spread(mean.astype(BF), ("y", "zl"), rolled((Y, Y0), (ZL, 0)))
+    got = spread(mean.astype(BF), gather_groups())
     slot_in = got.reshape(Y, ZL, groups, width).transpose(2, 0, 1, 3).reshape(groups, own, depth)
 
     hidden = jax.nn.gelu(jnp.einsum("bed,edf->bef", slot_in, w_in, preferred_element_type=F32)).astype(BF)
@@ -172,17 +202,17 @@
 
     pieces = partial_out.reshape(groups, Y, ZL, width).transpose(1, 2, 0, 3).reshape(Y * ZL * groups, width)
     total = jnp.sum(scatter(pieces).astype(F32), axis=0).astype(BF)
-    got = spread(total, "zh", rolled((ZH, H0)))
+    got = spread(total, long_groups(LONG_OUT))
     total = jnp.sum(got.astype(F32), axis=0).astype(BF)
-    got = spread(total, ("y", "zl"), rolled((Y, Y0), (ZL, 0)))
+    got = spread(total, gather_groups())
     slot_out = got.reshape(Y, ZL, groups, width).transpose(0, 2, 1, 3).reshape(slots, depth)
 
     return mix(combine, slot_out)[None]
 
 
 def solution(mesh):
-    fine = Mesh(mesh.devices.reshape(Y, ZH, ZL, X, C), ("y", "zh", "zl", "x", "c"))
-    ctx, exp = ("y", "zh", "zl"), ("x", "c")
+    fine = Mesh(mesh.devices.reshape(Y, Z, X, C), AXES)
+    ctx, exp = AXES[:2], AXES[2:]
     placed = (P(exp, ctx, None), P(), P(exp, None, ctx), P(exp, ctx, None))
     return jax.shard_map(
         on_device, mesh=fine, in_specs=placed, out_specs=P(exp, ctx, None), check_vma=False

time: 89.3 us -> 88 us (0.985)
  blocking collectives: 83.5 us -> 82 us
    all_to_all x6, blocking collectives: 83.5 us -> 82 us  [exchange(): lax.all_to_all(pieces, AXES, 0, 0, tiled=True, axis_index_groups=groups)]
where the time goes in v12:
time: 88 us; the launch traced here: 87.5 us
  blocking collectives  82 us (93%)
  Pallas kernels  3.73 us (4%)
    all_to_all x6, blocking collectives, exchange(): lax.all_to_all(pieces, AXES, 0, 0, tiled=True, axis_index_groups=groups)  82 us
    pallas_call x1, Pallas kernels, slot_sums(): pl.pallas_call(functools.partial(slot_kernel, groups), out_shape=(jax.Sha...  2.37 us

profile of v12, /device:TPU:6, one launch (start us, length us, event | category | flops | bytes accessed | tf_op | source)
XLA Modules:
  0.0 87.5 jit_solution(8709466519007005058)
XLA Ops:
  0.0 0.0 copy-start
  0.0 0.0 copy-start.1
  0.0 2.4 %slot_sums.1 = (bf16[64,768]{1,0:T(8,128)(2,1)S(1)}, bf16[32,512]{1,0:T(8,128)(2,1)S(1)}) custom-call(bf16[512,1280]{1,0:T(8,128)(2,1)} %bitcast.39, bf16[32,1280]{1,0:T(8,128)(2,1)} %bitcast.42), custom_call_target="tpu_custom_call" | custom-call | tf_op jit(solution)/shard_map/slot_sums/pallas_call | solution.py:105
  2.4 16.4 %all_to_all.30 = bf16[64,2,384]{2,1,0:T(2,128)(2,1)S(1)} all-to-all(bf16[64,2,384]{2,1,0:T(2,128)(2,1)S(1)} %reshape.117), channel_id=1, replica_groups={{391,390,385,384,387,386,389,388,399,398,393,392,395,394,397,396,7,6,1,..., dimensions={0} | all-to-all | bytes 196608 | tf_op jit(solution)/shard_map/all_to_all | solution.py:173
  18.8 0.1 reshape.118
  18.9 0.1 convert_reduce_fusion
  19.0 0.1 multiply_reduce_fusion.1
  19.1 0.1 divide_convert_fusion.1
  19.2 0.1 copy.13
  19.3 20.1 %all_to_all.31 = bf16[8,8,768]{2,1,0:T(8,128)(2,1)S(1)} all-to-all(bf16[8,8,768]{2,1,0:T(8,128)(2,1)S(1)} %broadcast_in_dim.10), channel_id=1, replica_groups={{88,104,120,0,16,32,48,72},{89,105,121,1,17,33,49,73},{90,106,122,2,18,..., dimensions={0} | all-to-all | bytes 196608 | tf_op jit(solution)/shard_map/all_to_all | solution.py:173
  39.4 0.1 copy.12
  39.6 0.1 multiply_reduce_fusion
  39.7 0.1 divide_convert_fusion
  39.8 8.7 %all_to_all.32 = bf16[8,8,640]{2,1,0:T(8,128)(2,1)S(1)} all-to-all(bf16[8,8,640]{2,1,0:T(8,128)(2,1)S(1)} %broadcast_in_dim.11), channel_id=1, replica_groups={{384,392,0,8,128,136,256,264},{385,393,1,9,129,137,257,265},{386,394,2,..., dimensions={0} | all-to-all | bytes 163840 | tf_op jit(solution)/shard_map/all_to_all | solution.py:173
  48.4 0.0 copy-done
  48.4 0.0 copy-done.1
  48.4 0.5 convolution_convert_fusion
  48.9 0.1 reshape_reshape.3
  49.1 11.9 %all_to_all.33 = bf16[64,2,320]{2,1,0:T(2,128)(2,1)S(1)} all-to-all(bf16[64,2,320]{2,1,0:T(2,128)(2,1)S(1)} %reshape_reshape.3), channel_id=1, replica_groups={{391,390,385,384,387,386,389,388,399,398,393,392,395,394,397,396,7,6,1,..., dimensions={0} | all-to-all | bytes 163840 | tf_op jit(solution)/shard_map/all_to_all | solution.py:173
  61.0 0.1 reshape.122
  61.2 16.3 %all_to_all.34 = bf16[8,8,640]{2,1,0:T(8,128)(2,1)S(1)} all-to-all(bf16[8,8,640]{2,1,0:T(8,128)(2,1)S(1)} %broadcast_in_dim.12), channel_id=1, replica_groups={{72,88,104,120,0,16,32,48},{73,89,105,121,1,17,33,49},{74,90,106,122,2,..., dimensions={0} | all-to-all | bytes 163840 | tf_op jit(solution)/shard_map/all_to_all | solution.py:173
  77.5 8.7 %all_to_all.35 = bf16[8,8,640]{2,1,0:T(8,128)(2,1)S(1)} all-to-all(bf16[8,8,640]{2,1,0:T(8,128)(2,1)S(1)} %broadcast_in_dim.13), channel_id=1, replica_groups={{384,392,0,8,128,136,256,264},{385,393,1,9,129,137,257,265},{386,394,2,..., dimensions={0} | all-to-all | bytes 163840 | tf_op jit(solution)/shard_map/all_to_all | solution.py:173
  86.1 1.4 %mix.1 = bf16[512,1280]{1,0:T(8,128)(2,1)} custom-call(bf16[32,512]{1,0:T(8,128)(2,1)S(1)} %get-tuple-element.7.combine_ref, bf16[32,1280]{1,0:T(8,128)(2,1)S(1)} %bitcast.38), custom_call_target="tpu_custom_call" | custom-call | tf_op jit(solution)/shard_map/mix/pallas_call | solution.py:138
  (16 shorter events, 0.2 us)
Async XLA Ops:
  0.0 48.4 %copy-start = (bf16[4,80,1280]{2,1,0:T(8,128)(2,1)S(1)}, bf16[4,80,1280]{2,1,0:T(8,128)(2,1)}, u32[]{:S(2)}) copy-start(bf16[4,80,1280]{2,1,0:T(8,128)(2,1)} %param.7) | copy-start | bytes 2457604
  0.0 48.4 %copy-start.1 = (bf16[4,1280,80]{1,2,0:T(8,128)(2,1)S(1)}, bf16[4,1280,80]{1,2,0:T(8,128)(2,1)}, u32[]{:S(2)}) copy-start(bf16[4,1280,80]{1,2,0:T(8,128)(2,1)} %param.6) | copy-start | bytes 2457604

commit v13 on v12

--- a/solution.py
+++ b/solution.py
@@ -161,7 +161,7 @@
 
 def merged(pieces, width):
     mean = pieces[..., :width].astype(F32)
-    lse = jnp.sum(pieces[..., width : width + 3].astype(F32), axis=-1)
+    lse = jnp.sum(pieces[..., width:].astype(F32), axis=-1)
     top = jnp.max(lse, axis=0)
     weight = jnp.exp(lse - top)
     total = jnp.sum(weight, axis=0)

time: 88 us -> 87.9 us (level)
  no operation moved by 1% of the time
where the time goes in v13:
time: 87.9 us; the launch traced here: 87.5 us
  blocking collectives  82 us (93%)
  Pallas kernels  3.74 us (4%)
    all_to_all x6, blocking collectives, exchange(): lax.all_to_all(pieces, AXES, 0, 0, tiled=True, axis_index_groups=groups)  82 us
    pallas_call x1, Pallas kernels, slot_sums(): pl.pallas_call(functools.partial(slot_kernel, groups), out_shape=(jax.Sha...  2.37 us

profile of v13, /device:TPU:6, one launch (start us, length us, event | category | flops | bytes accessed | tf_op | source)
XLA Modules:
  0.0 87.5 jit_solution(13051403762090387519)
XLA Ops:
  0.0 0.0 copy-start
  0.0 0.0 copy-start.1
  0.0 2.4 %slot_sums.1 = (bf16[64,768]{1,0:T(8,128)(2,1)S(1)}, bf16[32,512]{1,0:T(8,128)(2,1)S(1)}) custom-call(bf16[512,1280]{1,0:T(8,128)(2,1)} %bitcast.39, bf16[32,1280]{1,0:T(8,128)(2,1)} %bitcast.42), custom_call_target="tpu_custom_call" | custom-call | tf_op jit(solution)/shard_map/slot_sums/pallas_call | solution.py:105
  2.4 16.4 %all_to_all.30 = bf16[64,2,384]{2,1,0:T(2,128)(2,1)S(1)} all-to-all(bf16[64,2,384]{2,1,0:T(2,128)(2,1)S(1)} %reshape.117), channel_id=1, replica_groups={{391,390,385,384,387,386,389,388,399,398,393,392,395,394,397,396,7,6,1,..., dimensions={0} | all-to-all | bytes 196608 | tf_op jit(solution)/shard_map/all_to_all | solution.py:173
  18.8 0.1 reshape.118
  18.9 0.1 convert_reduce_fusion.1
  19.0 0.1 multiply_reduce_fusion.1
  19.1 0.1 divide_convert_fusion.1
  19.2 0.1 copy.7
  19.3 20.1 %all_to_all.31 = bf16[8,8,768]{2,1,0:T(8,128)(2,1)S(1)} all-to-all(bf16[8,8,768]{2,1,0:T(8,128)(2,1)S(1)} %broadcast_in_dim.10), channel_id=1, replica_groups={{88,104,120,0,16,32,48,72},{89,105,121,1,17,33,49,73},{90,106,122,2,18,..., dimensions={0} | all-to-all | bytes 196608 | tf_op jit(solution)/shard_map/all_to_all | solution.py:173
  39.4 0.1 convert_reduce_fusion
  39.5 0.1 multiply_reduce_fusion
  39.6 0.1 divide_convert_fusion
  39.7 8.7 %all_to_all.32 = bf16[8,8,640]{2,1,0:T(8,128)(2,1)S(1)} all-to-all(bf16[8,8,640]{2,1,0:T(8,128)(2,1)S(1)} %broadcast_in_dim.11), channel_id=1, replica_groups={{384,392,0,8,128,136,256,264},{385,393,1,9,129,137,257,265},{386,394,2,..., dimensions={0} | all-to-all | bytes 163840 | tf_op jit(solution)/shard_map/all_to_all | solution.py:173
  48.4 0.0 copy-done
  48.4 0.0 copy-done.1
  48.4 0.5 convolution_convert_fusion
  48.9 0.1 reshape_reshape.3
  49.0 11.9 %all_to_all.33 = bf16[64,2,320]{2,1,0:T(2,128)(2,1)S(1)} all-to-all(bf16[64,2,320]{2,1,0:T(2,128)(2,1)S(1)} %reshape_reshape.3), channel_id=1, replica_groups={{391,390,385,384,387,386,389,388,399,398,393,392,395,394,397,396,7,6,1,..., dimensions={0} | all-to-all | bytes 163840 | tf_op jit(solution)/shard_map/all_to_all | solution.py:173
  60.9 0.1 reshape.122
  61.1 16.3 %all_to_all.34 = bf16[8,8,640]{2,1,0:T(8,128)(2,1)S(1)} all-to-all(bf16[8,8,640]{2,1,0:T(8,128)(2,1)S(1)} %broadcast_in_dim.12), channel_id=1, replica_groups={{72,88,104,120,0,16,32,48},{73,89,105,121,1,17,33,49},{74,90,106,122,2,..., dimensions={0} | all-to-all | bytes 163840 | tf_op jit(solution)/shard_map/all_to_all | solution.py:173
  77.4 8.7 %all_to_all.35 = bf16[8,8,640]{2,1,0:T(8,128)(2,1)S(1)} all-to-all(bf16[8,8,640]{2,1,0:T(8,128)(2,1)S(1)} %broadcast_in_dim.13), channel_id=1, replica_groups={{384,392,0,8,128,136,256,264},{385,393,1,9,129,137,257,265},{386,394,2,..., dimensions={0} | all-to-all | bytes 163840 | tf_op jit(solution)/shard_map/all_to_all | solution.py:173
  86.1 1.4 %mix.1 = bf16[512,1280]{1,0:T(8,128)(2,1)} custom-call(bf16[32,512]{1,0:T(8,128)(2,1)S(1)} %get-tuple-element.7.combine_ref, bf16[32,1280]{1,0:T(8,128)(2,1)S(1)} %bitcast.38), custom_call_target="tpu_custom_call" | custom-call | tf_op jit(solution)/shard_map/mix/pallas_call | solution.py:138
  (14 shorter events, 0.2 us)
Async XLA Ops:
  0.0 48.4 %copy-start = (bf16[4,80,1280]{2,1,0:T(8,128)(2,1)S(1)}, bf16[4,80,1280]{2,1,0:T(8,128)(2,1)}, u32[]{:S(2)}) copy-start(bf16[4,80,1280]{2,1,0:T(8,128)(2,1)} %param.7) | copy-start | bytes 2457604
  0.0 48.4 %copy-start.1 = (bf16[4,1280,80]{1,2,0:T(8,128)(2,1)S(1)}, bf16[4,1280,80]{1,2,0:T(8,128)(2,1)}, u32[]{:S(2)}) copy-start(bf16[4,1280,80]{1,2,0:T(8,128)(2,1)} %param.6) | copy-start | bytes 2457604

commit v14 on v12

--- a/solution.py
+++ b/solution.py
@@ -201,7 +201,8 @@
     partial_out = jnp.einsum("bef,efd->bed", hidden, w_out, preferred_element_type=F32).astype(BF)
 
     pieces = partial_out.reshape(groups, Y, ZL, width).transpose(1, 2, 0, 3).reshape(Y * ZL * groups, width)
-    total = jnp.sum(scatter(pieces).astype(F32), axis=0).astype(BF)
+    pieces = jnp.pad(pieces, ((0, 0), (0, EXTRA)))
+    total = jnp.sum(scatter(pieces)[..., :width].astype(F32), axis=0).astype(BF)
     got = spread(total, long_groups(LONG_OUT))
     total = jnp.sum(got.astype(F32), axis=0).astype(BF)
     got = spread(total, gather_groups())

time: 88 us -> 87.9 us (level)
  no operation moved by 1% of the time
where the time goes in v14:
time: 87.9 us; the launch traced here: 87.4 us
  blocking collectives  82 us (93%)
  Pallas kernels  3.73 us (4%)
    all_to_all x6, blocking collectives, exchange(): lax.all_to_all(pieces, AXES, 0, 0, tiled=True, axis_index_groups=groups)  82 us
    pallas_call x1, Pallas kernels, slot_sums(): pl.pallas_call(functools.partial(slot_kernel, groups), out_shape=(jax.Sha...  2.37 us

profile of v14, /device:TPU:6, one launch (start us, length us, event | category | flops | bytes accessed | tf_op | source)
XLA Modules:
  0.0 87.4 jit_solution(13084290736793442602)
XLA Ops:
  0.0 0.0 copy-start
  0.0 0.0 copy-start.1
  0.0 2.4 %slot_sums.1 = (bf16[64,768]{1,0:T(8,128)(2,1)S(1)}, bf16[32,512]{1,0:T(8,128)(2,1)S(1)}) custom-call(bf16[512,1280]{1,0:T(8,128)(2,1)} %bitcast.39, bf16[32,1280]{1,0:T(8,128)(2,1)} %bitcast.42), custom_call_target="tpu_custom_call" | custom-call | tf_op jit(solution)/shard_map/slot_sums/pallas_call | solution.py:105
  2.4 16.4 %all_to_all.30 = bf16[64,2,384]{2,1,0:T(2,128)(2,1)S(1)} all-to-all(bf16[64,2,384]{2,1,0:T(2,128)(2,1)S(1)} %reshape.123), channel_id=1, replica_groups={{391,390,385,384,387,386,389,388,399,398,393,392,395,394,397,396,7,6,1,..., dimensions={0} | all-to-all | bytes 196608 | tf_op jit(solution)/shard_map/all_to_all | solution.py:173
  18.8 0.1 reshape.124
  18.9 0.1 convert_reduce_fusion
  19.0 0.1 multiply_reduce_fusion.1
  19.1 0.1 divide_convert_fusion.1
  19.2 0.1 copy.13
  19.3 20.1 %all_to_all.31 = bf16[8,8,768]{2,1,0:T(8,128)(2,1)S(1)} all-to-all(bf16[8,8,768]{2,1,0:T(8,128)(2,1)S(1)} %broadcast_in_dim.10), channel_id=1, replica_groups={{88,104,120,0,16,32,48,72},{89,105,121,1,17,33,49,73},{90,106,122,2,18,..., dimensions={0} | all-to-all | bytes 196608 | tf_op jit(solution)/shard_map/all_to_all | solution.py:173
  39.4 0.1 copy.12
  39.6 0.1 multiply_reduce_fusion
  39.7 0.1 divide_convert_fusion
  39.8 8.7 %all_to_all.32 = bf16[8,8,640]{2,1,0:T(8,128)(2,1)S(1)} all-to-all(bf16[8,8,640]{2,1,0:T(8,128)(2,1)S(1)} %broadcast_in_dim.11), channel_id=1, replica_groups={{384,392,0,8,128,136,256,264},{385,393,1,9,129,137,257,265},{386,394,2,..., dimensions={0} | all-to-all | bytes 163840 | tf_op jit(solution)/shard_map/all_to_all | solution.py:173
  48.4 0.0 copy-done
  48.4 0.0 copy-done.1
  48.4 0.5 convolution_convert_fusion
  49.0 11.9 %all_to_all.33 = bf16[64,2,384]{2,1,0:T(2,128)(2,1)S(1)} all-to-all(bf16[64,2,384]{2,1,0:T(2,128)(2,1)S(1)} %reshape.129), channel_id=1, replica_groups={{391,390,385,384,387,386,389,388,399,398,393,392,395,394,397,396,7,6,1,..., dimensions={0} | all-to-all | bytes 196608 | tf_op jit(solution)/shard_map/all_to_all | solution.py:173
  60.9 0.1 reshape.130
  61.0 16.3 %all_to_all.34 = bf16[8,8,640]{2,1,0:T(8,128)(2,1)S(1)} all-to-all(bf16[8,8,640]{2,1,0:T(8,128)(2,1)S(1)} %broadcast_in_dim.12), channel_id=1, replica_groups={{72,88,104,120,0,16,32,48},{73,89,105,121,1,17,33,49},{74,90,106,122,2,..., dimensions={0} | all-to-all | bytes 163840 | tf_op jit(solution)/shard_map/all_to_all | solution.py:173
  77.3 8.7 %all_to_all.35 = bf16[8,8,640]{2,1,0:T(8,128)(2,1)S(1)} all-to-all(bf16[8,8,640]{2,1,0:T(8,128)(2,1)S(1)} %broadcast_in_dim.13), channel_id=1, replica_groups={{384,392,0,8,128,136,256,264},{385,393,1,9,129,137,257,265},{386,394,2,..., dimensions={0} | all-to-all | bytes 163840 | tf_op jit(solution)/shard_map/all_to_all | solution.py:173
  86.0 1.4 %mix.1 = bf16[512,1280]{1,0:T(8,128)(2,1)} custom-call(bf16[32,512]{1,0:T(8,128)(2,1)S(1)} %get-tuple-element.7.combine_ref, bf16[32,1280]{1,0:T(8,128)(2,1)S(1)} %bitcast.38), custom_call_target="tpu_custom_call" | custom-call | tf_op jit(solution)/shard_map/mix/pallas_call | solution.py:138
  (18 shorter events, 0.3 us)
Async XLA Ops:
  0.0 48.4 %copy-start = (bf16[4,80,1280]{2,1,0:T(8,128)(2,1)S(1)}, bf16[4,80,1280]{2,1,0:T(8,128)(2,1)}, u32[]{:S(2)}) copy-start(bf16[4,80,1280]{2,1,0:T(8,128)(2,1)} %param.7) | copy-start | bytes 2457604
  0.0 48.4 %copy-start.1 = (bf16[4,1280,80]{1,2,0:T(8,128)(2,1)S(1)}, bf16[4,1280,80]{1,2,0:T(8,128)(2,1)}, u32[]{:S(2)}) copy-start(bf16[4,1280,80]{1,2,0:T(8,128)(2,1)} %param.6) | copy-start | bytes 2457604
